TPU v7x, 32 devices: a whole 2x2x4 slice. The times are simulated.
32 devices in a mesh: seq: 16 (over z, y, core), row: 2 (over x).
Axes of the slice: x: 2, y: 2, z: 4, core: 2. Of those that a mesh axis runs over, the one named last changes fastest.
Arguments:
- layer_input: bfloat16 [2, 16384, 384], P('row', 'seq'), may hold values from -6 to 6
- segment_ids: int32 [2, 16384], P('row', 'seq'), may hold values from 0 to 63, never falling along the last dimension, each value on 1 to 512 neighbouring positions
- out_grad: bfloat16 [2, 16384, 384], P('row', 'seq'), may hold values from -6 to 6
- weights: float32 [1971840], P(('seq', 'row')), may hold values from -3 to 3
- momentum: float32 [1971840], P(('seq', 'row')), may hold values from -271.529 to 271.529
- average: float32 [1971840], P(('seq', 'row')), may hold values from -3 to 3
Outputs:
- block_output: bfloat16 [2, 16384, 384], P('row', 'seq')
- input_grad: float32 [2, 16384, 384], P('row', 'seq')
- weight_grad: float32 [1971840], P(('seq', 'row'))
- new_momentum: float32 [1971840], P(('seq', 'row'))
- new_average: float32 [1971840], P(('seq', 'row'))
- new_weights: float32 [1971840], P(('seq', 'row'))
- weight_copy: bfloat16 [1971840], P(('seq', 'row'))
Inputs may be any that keep to these rules, and one draw needn't show every extreme that they name: `segment_ids`: ids never fall along a row; every document holds 1 to 512 tokens and one of each row holds exactly 512.
All inputs are finite; a program needn't handle non-finite values.
Results may differ from a plain program's by a relative error of at most 0.012.
The roundings to bfloat16 on the way count: a program that leaves them out, or rounds other values in their place, can miss the bound.
Values may be sent and summed in bfloat16 or wider, within the bound.
A program may use at most 128 MiB of HBM per device.

v0:
```python
import functools
import itertools
import math

import jax
import jax.numpy as jnp
from jax import lax
from jax.experimental import pallas as pl
from jax.experimental.pallas import tpu as pltpu
from jax.sharding import PartitionSpec as P

D = 384
HEADS = 6
HEAD_DIM = 64
FF = 1536
SPAN = 256
PAIRS = HEADS // 2
NB = 5
EPSILON = 1e-07
bf = jnp.bfloat16
f32 = jnp.float32


MESH = pl.DeviceIdType.MESH
GROUP = 2048


class Grid:
    def __init__(self, seq, row):
        half = seq // 2
        wide = 1
        while wide * wide * 4 <= half:
            wide *= 2
        self.size = {"z": half // wide, "y": wide, "x": row}
        self.seq, self.row, self.count = seq, row, seq * row

    def here(self):
        s, x = lax.axis_index("seq"), lax.axis_index("row")
        y_size = self.size["y"]
        return {"z": s // (2 * y_size), "y": (s // 2) % y_size, "c": s % 2, "x": x}

    def seq_of(self, p):
        return (p["z"] * self.size["y"] + p["y"]) * 2 + p["c"]

    def flat(self, p):
        return self.seq_of(p) * self.row + p["x"]

    def device(self, p):
        return {"seq": self.seq_of(p), "row": p["x"]}

    def plane(self, p):
        return (p["z"] * self.size["y"] + p["y"]) * self.row + p["x"]

    def offsets(self, order):
        choices = []
        for axis in order:
            n = self.size[axis]
            if n == 2:
                choices.append([0, "f"])
            else:
                choices.append([0] + [sign * d for d in range(1, n) for sign in (-1, 1)])
        hops = lambda off: sum(1 if o == "f" else abs(o) for o in off)
        return sorted(itertools.product(*choices), key=hops)


def both(conds):
    out = None
    for cond in conds:
        if cond is not None:
            out = cond if out is None else jnp.logical_and(out, cond)
    return out


def guarded(cond, fn):
    if cond is None:
        fn()
    else:
        pl.when(cond)(fn)


def source_of(grid, p, order, off):
    o, conds = dict(p), []
    for axis, d in zip(order, off):
        if d == "f":
            o[axis] = 1 - p[axis]
        elif d != 0:
            o[axis] = p[axis] + d
            conds.append(p[axis] + d >= 0 if d < 0 else p[axis] + d < grid.size[axis])
    return o, both(conds)


def parent_of(grid, p, order, off):
    last = max((i for i, d in enumerate(off) if d != 0), default=None)
    if last is None:
        return None, None
    q, axis, d = dict(p), order[last], off[last]
    if d == "f":
        q[axis] = 1 - p[axis]
        return q, axis + "0"
    q[axis] = p[axis] + (1 if d > 0 else -1)
    return q, axis + ("+" if d > 0 else "-")


def children_of(grid, p, order, off):
    last = max((i for i, d in enumerate(off) if d != 0), default=None)
    found = []
    if last is not None and off[last] != "f":
        axis, away = order[last], (-1 if off[last] > 0 else 1)
        q = dict(p)
        q[axis] = p[axis] + away
        found.append((axis + ("+" if away > 0 else "-"), q, p[axis] > 0 if away < 0 else p[axis] < grid.size[axis] - 1))
    for axis in order[0 if last is None else last + 1 :]:
        if grid.size[axis] == 2:
            q = dict(p)
            q[axis] = 1 - p[axis]
            found.append((axis + "0", q, None))
        elif grid.size[axis] > 2:
            for sign in (1, -1):
                q = dict(p)
                q[axis] = p[axis] + sign
                found.append((axis + ("+" if sign > 0 else "-"), q, p[axis] > 0 if sign < 0 else p[axis] < grid.size[axis] - 1))
    return found


def neighbours_of(grid, p):
    found = []
    for axis in ("z", "y", "x"):
        found += children_of(grid, p, (axis,), (0,))
    sibling = dict(p)
    sibling["c"] = 1 - p["c"]
    found.append(("c0", sibling, None))
    return found


def enter(grid, p, extra=()):
    sem = pltpu.get_barrier_semaphore()
    total = jnp.int32(0)
    for name, q, cond in neighbours_of(grid, p) + list(extra):
        guarded(cond, lambda q=q: pl.semaphore_signal(sem, inc=1, device_id=grid.device(q), device_id_type=MESH))
        total = total + (1 if cond is None else cond.astype(jnp.int32))
    pl.semaphore_wait(sem, total)


def orders_of(groups):
    return (("z", "y", "x"), ("x", "z", "y")) if groups >= 8 else (("z", "y", "x"),)


def spans(groups):
    if groups < 8:
        return ((0, 16 * groups),)
    first = (groups * 20 + 16) // 32
    return ((0, 16 * first), (16 * first, 16 * (groups - first)))


class Gather:
    def __init__(self, grid, p, slots, send_sem, recv_sem, groups):
        self.grid, self.p, self.slots = grid, p, slots
        self.send_sem, self.recv_sem, self.groups = send_sem, recv_sem, groups
        self.sends, self.used = [], 0

    def copy(self, part, k, q, index):
        start, rows = spans(self.groups)[part]
        block = self.slots.at[k, pl.ds(start, rows), :]
        return pltpu.make_async_remote_copy(
            src_ref=block, dst_ref=block, send_sem=self.send_sem.at[index], recv_sem=self.recv_sem.at[part, k],
            device_id=self.grid.device(q), device_id_type=MESH)

    def arrived(self, part, k):
        start, rows = spans(self.groups)[part]
        block = self.slots.at[k, pl.ds(start, rows), :]
        pltpu.make_async_remote_copy(
            src_ref=block, dst_ref=block, send_sem=self.send_sem.at[0], recv_sem=self.recv_sem.at[part, k],
            device_id=self.grid.device(self.p), device_id_type=MESH).wait_recv()

    def run(self):
        grid, p = self.grid, self.p
        steps = []
        for part, order in enumerate(orders_of(self.groups)):
            for off in grid.offsets(order):
                steps.append((sum(1 if o == "f" else abs(o) for o in off), part, order, off))
        steps.sort(key=lambda item: item[:2])
        sibling = dict(p)
        sibling["c"] = 1 - p["c"]
        finish = []
        for hops, part, order, off in steps:
            o, cond = source_of(grid, p, order, off)
            k = grid.flat(o)
            targets = children_of(grid, p, order, off) + [("c0", sibling, None)]
            indices = [self.used + i for i in range(len(targets))]
            self.used += len(targets)

            def step(part=part, k=k, targets=targets, indices=indices, own=hops == 0):
                if not own:
                    self.arrived(part, k)
                for (name, q, when), index in zip(targets, indices):
                    guarded(when, lambda q=q, index=index: self.copy(part, k, q, index).start())

            guarded(cond, step)

            def end(part=part, k=k, targets=targets, indices=indices):
                for (name, q, when), index in zip(targets, indices):
                    guarded(when, lambda q=q, index=index: self.copy(part, k, q, index).wait_send())

            finish.append((cond, end))
        for part, order in enumerate(orders_of(self.groups)):
            for off in grid.offsets(order):
                o, cond = source_of(grid, sibling, order, off)
                guarded(cond, lambda part=part, k=grid.flat(o): self.arrived(part, k))
        for cond, end in finish:
            guarded(cond, end)

def count_sends(grid, groups):
    fake = {"z": jnp.int32(0), "y": jnp.int32(0), "x": jnp.int32(0), "c": jnp.int32(0)}
    return sum(len(children_of(grid, fake, order, off)) + 1 for order in orders_of(groups) for off in grid.offsets(order))


OPPOSITE = {"+": "-", "-": "+", "0": "0"}


def direction_names(grid):
    names = ["c0"]
    for axis in ("z", "y", "x"):
        if grid.size[axis] == 2:
            names.append(axis + "0")
        elif grid.size[axis] > 2:
            names += [axis + "+", axis + "-"]
    return names


class Scatter:
    def __init__(self, grid, p, flat, first_row, kids, outgoing, total, send_sem, recv_sem, groups):
        self.grid, self.p, self.flat, self.first_row = grid, p, flat, first_row
        self.kids, self.outgoing, self.total = kids, outgoing, total
        self.send_sem, self.recv_sem, self.groups = send_sem, recv_sem, groups
        self.names = direction_names(grid)

    def incoming(self, part, name, place):
        start, rows = spans(self.groups)[part]
        return self.kids.at[self.names.index(name), place, pl.ds(start, rows), :]

    def transfer(self, source, part, name, place, q, send):
        return pltpu.make_async_remote_copy(
            src_ref=source, dst_ref=self.incoming(part, name, place), send_sem=self.send_sem.at[send],
            recv_sem=self.recv_sem.at[part, self.names.index(name), place], device_id=self.grid.device(q), device_id_type=MESH)

    def arrived(self, part, name, place):
        block = self.incoming(part, name, place)
        pltpu.make_async_remote_copy(
            src_ref=block, dst_ref=block, send_sem=self.send_sem.at[0],
            recv_sem=self.recv_sem.at[part, self.names.index(name), place],
            device_id=self.grid.device(self.p), device_id_type=MESH).wait_recv()

    def run(self, result):
        grid, p = self.grid, self.p
        sibling = dict(p)
        sibling["c"] = 1 - p["c"]
        steps = []
        for part, order in enumerate(orders_of(self.groups)):
            for off in grid.offsets(order):
                steps.append((-sum(1 if o == "f" else abs(o) for o in off), part, order, off))
        steps.sort(key=lambda item: item[:2])
        used, finish = 0, []
        for hops, part, order, off in steps:
            o, cond = source_of(grid, sibling, order, off)
            start, rows = spans(self.groups)[part]

            def give(part=part, o=o, index=used, start=start, rows=rows):
                block = self.flat.at[pl.ds(pl.multiple_of(self.first_row(grid.flat(o)) + start, 16), rows), :]
                return self.transfer(block, part, "c0", grid.plane(o), sibling, index)

            guarded(cond, lambda give=give: give().start())
            finish.append((cond, lambda give=give: give().wait_send()))
            used += 1
        for hops, part, order, off in steps:
            o, cond = source_of(grid, p, order, off)
            place, k = grid.plane(o), grid.flat(o)
            start, rows = spans(self.groups)[part]
            kids = children_of(grid, p, order, off)
            parent, side = parent_of(grid, p, order, off)

            def push(part=part, place=place, parent=parent, side=side, index=used, start=start, rows=rows):
                block = self.outgoing.at[place, pl.ds(start, rows), :]
                return self.transfer(block, part, side[0] + OPPOSITE[side[1]], place, parent, index)

            def step(part=part, place=place, k=k, kids=kids, parent=parent, start=start, rows=rows, push=push):
                self.arrived(part, "c0", place)
                mine = self.flat[pl.ds(pl.multiple_of(self.first_row(k) + start, 16), rows), :].astype(f32)
                self.total[0:rows, :] = mine + self.incoming(part, "c0", place)[...].astype(f32)
                for name, q, when in kids:

                    def add(name=name):
                        self.arrived(part, name, place)
                        self.total[0:rows, :] += self.incoming(part, name, place)[...].astype(f32)

                    guarded(when, add)
                if parent is None:
                    result[pl.ds(start, rows), :] = self.total[0:rows, :]
                else:
                    self.outgoing[place, pl.ds(start, rows), :] = self.total[0:rows, :].astype(bf)
                    push().start()

            guarded(cond, step)
            if parent is not None:
                finish.append((cond, lambda push=push: push().wait_send()))
                used += 1
        for cond, end in finish:
            guarded(cond, end)


def scatter_sends(grid, groups):
    return 2 * sum(len(grid.offsets(order)) for order in orders_of(groups))


def shard_groups(shard, count):
    first = [shard * k // GROUP for k in range(count)]
    groups = max(-(-shard * (k + 1) // GROUP) - first[k] for k in range(count))
    return first, max(groups, 2)


def flat_rows(shard, count):
    first, groups = shard_groups(shard, count)
    return 16 * (first[-1] + groups)


def layer_pieces():
    square, vector_of = (D, D), (D,)
    return (
        ("query_w", square), ("key_w", square), ("value_w", square), ("output_w", square), ("up_w", (D, FF)), ("down_w", (FF, D)),
        ("query_b", vector_of), ("key_b", vector_of), ("value_b", vector_of), ("output_b", vector_of), ("attn_gain", vector_of),
        ("attn_shift", vector_of), ("up_bias", (FF,)), ("down_bias", vector_of), ("ffn_gain", vector_of), ("ffn_shift", vector_of),
        ("rel_table", (2 * SPAN, D)), ("rel_gain", vector_of), ("rel_shift", vector_of),
    )


def matrix_rows():
    place, at = {}, 0
    for name, extent in layer_pieces():
        if len(extent) == 2:
            place[name] = (at // 128, extent[0], extent[1] // 128)
        else:
            place[name] = (at // 128, 1, extent[0] // 128)
        at += math.prod(extent)
    return place


MATRICES = ("query_w", "key_w", "value_w", "output_w", "up_w", "down_w", "rel_table")
VECTORS = tuple(name for name, extent in layer_pieces() if len(extent) == 1)
FEED_FIRST = matrix_rows()["output_w"][0]
FEED_ROWS = matrix_rows()["query_b"][0] - FEED_FIRST
USED_ROWS = sum(rows * pieces for _, rows, pieces in matrix_rows().values())


def vector_rows():
    place, at = {}, 0
    for name in VECTORS:
        wide = matrix_rows()[name][2]
        place[name] = (at, wide)
        at += wide
    return place, -(-at // 8) * 8


SC = 1.0/math.sqrt(3.0*HEAD_DIM)
LOG2E = 1.4426950408889634
NT=(((1,),(1,)),((),())); NN=(((1,),(0,)),((),())); TN=(((0,),(0,)),((),()))
def dot(a,b,d=NN): return lax.dot_general(a,b,d,preferred_element_type=f32)

def head_mask(rows, h):
    lane=lax.broadcasted_iota(jnp.int32,(rows,128),1)
    return (lane<64) if h==0 else (lane>=64)
def keep(x,h):
    return jnp.where(head_mask(x.shape[0],h), x, jnp.zeros_like(x))

def skew(A):
    return jnp.concatenate([pltpu.roll(A[8*g:8*g+8,:512],8*g+1,1,stride=1,stride_axis=0) for g in range(16)],axis=0)


def att_fwd_body(nblk, q_ref,k_ref,v_ref,krt_ref,qrt_ref,seg_ref,ctx_ref,p_ref,x_scr,bias_scr):
    row=lax.broadcasted_iota(jnp.int32,(128,128),0); lane=lax.broadcasted_iota(jnp.int32,(128,128),1)
    eye=(row==lane).astype(bf)
    def mk_bias(t,c):
        off=pl.multiple_of(t*128,128)
        sq=jnp.broadcast_to(seg_ref[0:1,pl.ds(pl.multiple_of(off+SPAN,128),128)],(128,128)).astype(f32).T
        for b in range(NB):
            sk=seg_ref[0:1,pl.ds(pl.multiple_of(off+128*b,128),128)].astype(f32)
            ok = sq==sk
            if b==0: ok = ok & (lane>=row)
            if b==NB-1: ok = ok & (lane<=row)
            bias_scr[t,:,128*b:128*b+128]=jnp.where(ok,0.0,-1e30).astype(f32)
        return c
    lax.fori_loop(0,nblk,mk_bias,0)
    def pair(p,c):
        def keyside(J):
            kj=k_ref[p,pl.ds(pl.multiple_of(jnp.minimum(J,nblk+3)*128,128),128),:]
            for h in range(2):
                C=dot(keep(kj,h),qrt_ref[p],NT)
                R=skew(C)
                x_scr[h,J,:,0:128]=jnp.where(lane>row,R[:,:128],C[:,512:]).astype(bf)
                x_scr[h,J,:,128:512]=R[:,128:].astype(bf)
                x_scr[h,J,:,512:640]=R[:,:128].astype(bf)
        def st(J,c):
            keyside(J); return c
        lax.fori_loop(0,5,st,0)
        def qblock(t,c):
            off=pl.multiple_of(t*128,128)
            qt=q_ref[p,pl.ds(off,128),:]
            kw=[k_ref[p,pl.ds(pl.multiple_of(off+128*b,128),128),:] for b in range(NB)]
            vw=v_ref[p,pl.ds(off,640),:]
            ctx=[]
            for h in range(2):
                qm=keep(qt,h)
                A=dot(qm,krt_ref[p],NT)
                R=skew(A)
                lhs=jnp.concatenate([qm,eye],axis=1)
                rhs=jnp.concatenate([jnp.concatenate([kw[b],x_scr[h,t+b,:,128*(4-b):128*(5-b)]],axis=1) for b in range(NB)],axis=0)
                S=dot(lhs,rhs,NT)
                Y=jnp.concatenate([jnp.where(lane>row,R[:,:128],A[:,512:]),R[:,128:],R[:,:128]],axis=1)
                S=S+Y+bias_scr[t]
                m=jnp.max(S,axis=1,keepdims=True)
                e=jnp.exp2((S-m)*(SC*LOG2E))
                s=jnp.sum(e,axis=1,keepdims=True)
                P=(e*(1.0/s)).astype(bf)
                p_ref[p,t,h]=P
                ctx.append(dot(P,vw,NN))
            ctx_ref[p,pl.ds(off,128),:]=jnp.where(lane<64,ctx[0],ctx[1]).astype(bf)
            keyside(c)
            return c+1
        lax.fori_loop(0,nblk,qblock,jnp.int32(5))
        return c
    lax.fori_loop(0,PAIRS,pair,0)

def unskew(Grev):
    return jnp.concatenate([pltpu.roll(Grev[8*g:8*g+8],384+8*g,1,stride=1,stride_axis=0) for g in range(16)],axis=0)

def unrev(x, J):
    hi=x.astype(bf); lo=(x-hi.astype(f32)).astype(bf)
    y=dot(J,jnp.concatenate([hi,lo],axis=1))
    return y[:,:128]+y[:,128:]

def att_bwd_body(nblk, q_ref,k_ref,v_ref,krt_ref,qrt_ref,dctx_ref,p_ref,dq_ref,dk_ref,dv_ref,dkr_ref,dqr_ref,gt_scr,dvt_scr):
    row=lax.broadcasted_iota(jnp.int32,(128,128),0); lane=lax.broadcasted_iota(jnp.int32,(128,128),1)
    JR=(row+lane==127).astype(bf)
    gt_scr[...]=jnp.zeros(gt_scr.shape,bf)
    zero=jnp.zeros((128,128),bf)
    def pair(p,c):
        dvt_scr[...]=jnp.zeros(dvt_scr.shape,f32)
        dkr_ref[p]=jnp.zeros((128,640),f32)
        dqr_ref[p]=jnp.zeros((128,640),f32)
        def qblock(t,J0):
            off=pl.multiple_of(t*128,128)
            qt=q_ref[p,pl.ds(off,128),:]
            qT=qt.T
            qTr=dot(qT,JR).astype(bf)
            dct=dctx_ref[p,pl.ds(off,128),:]
            dcT=dct.T
            kw=k_ref[p,pl.ds(off,640),:]
            vw=v_ref[p,pl.ds(off,640),:]
            krt=krt_ref[p]
            dq1=[]; dq2=[]
            for h in range(2):
                dp=dot(keep(dct,h),vw,NT)
                Pb=p_ref[p,t,h]
                Pf=Pb.astype(f32)
                w=Pf*dp
                inner=jnp.sum(w,axis=1,keepdims=True)
                G=(w-Pf*inner).astype(bf)
                Gd=jnp.where(lane==row,G[:,:128],zero)
                Gm=jnp.concatenate([jnp.where(lane>row,G[:,:128],G[:,512:]),G[:,128:512]],axis=1)
                Gu=unskew(dot(JR,Gm)).astype(bf)
                dq1.append(dot(jnp.concatenate([G,Gd],axis=1),jnp.concatenate([kw,krt[512:]],axis=0)))
                dq2.append(dot(Gu,krt[:512]))
                hs=slice(64*h,64*h+64)
                dkr_ref[p,hs,0:512]+=dot(qTr[hs],Gu)
                dkr_ref[p,hs,512:640]+=dot(qT[hs],Gd)
                dvt_scr[hs,pl.ds(off,640)]+=dot(dcT[hs],Pb)
                for b in range(NB):
                    gt_scr[h,J0+b,:,128*(4-b):128*(5-b)]=dot(JR,G[:,128*b:128*b+128],NT).astype(bf)
            dq=jnp.where(lane<64,dq1[0],dq1[1])+unrev(jnp.where(lane<64,dq2[0],dq2[1]),JR)
            dq_ref[p,pl.ds(off,128),:]=(SC*dq).astype(bf)
            return J0+1
        lax.fori_loop(0,nblk,qblock,jnp.int32(0))
        def kblock(J,c):
            off=pl.multiple_of(J*128,128)
            kj=k_ref[p,pl.ds(off,128),:]
            kT=kj.T
            kTr=dot(kT,JR).astype(bf)
            qw=jnp.concatenate([q_ref[p,pl.ds(pl.multiple_of(jnp.clip(J-4+w,0,nblk-1)*128,128),128),:] for w in range(NB)],axis=0)
            rhs=jnp.concatenate([qw,qrt_ref[p]],axis=0)
            dks=[]
            for h in range(2):
                GT=gt_scr[h,J]
                Gd=jnp.where(lane+row==127,GT[:,:128],zero)
                Gm=jnp.concatenate([jnp.where(lane+row>127,GT[:,:128],GT[:,512:]),GT[:,128:512]],axis=1).astype(f32)
                Gu=unskew(Gm).astype(bf)
                Gx=jnp.concatenate([Gu,Gd],axis=1)
                dks.append(dot(jnp.concatenate([GT,Gx],axis=1),rhs))
                hs=slice(64*h,64*h+64)
                dqr_ref[p,hs,:]+=dot(kTr[hs],Gx)
            dk_ref[p,pl.ds(off,128),:]=SC*unrev(jnp.where(lane<64,dks[0],dks[1]),JR)
            dv_ref[p,pl.ds(off,128),:]=dvt_scr[:,pl.ds(off,128)].T
            return c
        lax.fori_loop(0,nblk+4,kblock,0)
        dkr_ref[p]=SC*dkr_ref[p]
        dqr_ref[p]=SC*dqr_ref[p]
        return c
    lax.fori_loop(0,PAIRS,pair,0)

def att_bwd(q,k,v,krt,qrt,dctx,P):
    T=q.shape[1]; nblk=T//128; E=T+512
    return pl.pallas_call(functools.partial(att_bwd_body,nblk),
        out_shape=[jax.ShapeDtypeStruct((PAIRS,T,128),bf),jax.ShapeDtypeStruct((PAIRS,E,128),f32),jax.ShapeDtypeStruct((PAIRS,E,128),f32),
          jax.ShapeDtypeStruct((PAIRS,128,640),f32),jax.ShapeDtypeStruct((PAIRS,128,640),f32)],
        scratch_shapes=[pltpu.VMEM((2,nblk+4,128,640),bf),pltpu.VMEM((128,E),f32)],
        compiler_params=pltpu.CompilerParams(vmem_limit_bytes=48<<20),
    )(q,k,v,krt,qrt,dctx,P)


def vector(vec_ref, name):
    at, wide = vector_rows()[0][name]
    return jnp.concatenate([vec_ref[at + i : at + i + 1, :] for i in range(wide)], axis=1)


def put_vector(vec_ref, name, value):
    at, wide = vector_rows()[0][name]
    for i in range(wide):
        vec_ref[at + i : at + i + 1, :] = value[:, 128 * i : 128 * i + 128]


def add_vector(vec_ref, name, value):
    at, wide = vector_rows()[0][name]
    for i in range(wide):
        vec_ref[at + i : at + i + 1, :] += value[:, 128 * i : 128 * i + 128]


def normalized(values):
    centered = values - jnp.mean(values, axis=1, keepdims=True)
    inverse = lax.rsqrt(jnp.mean(centered * centered, axis=1, keepdims=True) + EPSILON)
    return centered * inverse, inverse


def norm_back(upstream, gain, unit, inverse):
    scaled = upstream * gain
    mean = jnp.mean(scaled, axis=1, keepdims=True)
    along = jnp.mean(scaled * unit, axis=1, keepdims=True)
    return inverse * (scaled - mean - unit * along)


def column_sum(values):
    return jnp.sum(values, axis=0, keepdims=True)


def reversal():
    row = lax.broadcasted_iota(jnp.int32, (128, 128), 0)
    lane = lax.broadcasted_iota(jnp.int32, (128, 128), 1)
    return (row + lane == 127).astype(bf)


def reversed_rows(values, JR):
    blocks = values.shape[0] // 128
    return jnp.concatenate([dot(JR, values[128 * b : 128 * b + 128]).astype(bf) for b in reversed(range(blocks))], axis=0)


def project_body(x_ref, query_w, key_w, value_w, table_ref, vec_ref, q_ref, k_ref, v_ref, krt_ref, qrt_ref, pos_ref):
    tokens = q_ref.shape[1]
    JR = reversal()
    unit, _ = normalized(table_ref[...].astype(f32))
    pos = (unit * vector(vec_ref, "rel_gain") + vector(vec_ref, "rel_shift")).astype(bf)
    pos_rev = reversed_rows(pos, JR)
    pos_ref[...] = pos_rev
    for w, b, out in ((key_w, "key_b", krt_ref), (query_w, "query_b", qrt_ref)):
        table = (dot(pos_rev, w[...]) + vector(vec_ref, b)).astype(bf)
        for p in range(PAIRS):
            out[p, 0:512, :] = table[:, 128 * p : 128 * p + 128]
            out[p, 512:640, :] = jnp.broadcast_to(table[0:1, 128 * p : 128 * p + 128], (128, 128))

    bias = {name: vector(vec_ref, name) for name in ("query_b", "key_b", "value_b")}

    def chunk(i, carry):
        rows = pl.ds(pl.multiple_of(i * 256, 256), 256)
        x = x_ref[rows, :]
        for w, b, out in ((key_w, "key_b", k_ref), (value_w, "value_b", v_ref)):
            y = (dot(x, w[...]) + bias[b]).astype(bf)
            for p in range(PAIRS):
                out[p, rows, :] = y[:, 128 * p : 128 * p + 128]
        return carry

    lax.fori_loop(0, x_ref.shape[0] // 256, chunk, 0)

    def own(i, carry):
        rows = pl.ds(pl.multiple_of(i * 256, 256), 256)
        x = x_ref[pl.ds(pl.multiple_of(i * 256 + SPAN, 256), 256), :]
        y = (dot(x, query_w[...]) + bias["query_b"]).astype(bf)
        for p in range(PAIRS):
            q_ref[p, rows, :] = y[:, 128 * p : 128 * p + 128]
        return carry

    lax.fori_loop(0, tokens // 256, own, 0)


SQRT_HALF = 0.7071067811865476
PHI_SCALE = 0.3989422804014327


def gelu_and_slope(u):
    cdf = 0.5 + 0.5 * lax.erf(u * SQRT_HALF)
    return u * cdf, cdf + u * (PHI_SCALE * jnp.exp(-0.5 * u * u))


def feed_body(x_ref, ctx_ref, og_ref, output_w, up_w, down_w, vec_ref, out_ref, dz1_ref, dctx_ref, wide, dvec_ref,
              ml_scr, dup_scr, act_scr, ddown_scr, dattn_scr, slope_scr):
    tokens = out_ref.shape[0]
    dvec_ref[...] = jnp.zeros(dvec_ref.shape, f32)
    vecs = {name: vector(vec_ref, name) for name in ("output_b", "attn_gain", "attn_shift", "up_bias", "down_bias", "ffn_gain", "ffn_shift")}
    C = 256

    def chunk(i, carry):
        rows = pl.ds(pl.multiple_of(i * C, C), C)
        h = x_ref[pl.ds(pl.multiple_of(i * C + SPAN, C), C), :].astype(f32)
        z1 = h + dot(jnp.concatenate([ctx_ref[p, rows, :] for p in range(PAIRS)], axis=1), output_w[...]) + vecs["output_b"]
        unit1, inv1 = normalized(z1)
        mid = unit1 * vecs["attn_gain"] + vecs["attn_shift"]
        ml = mid.astype(bf)
        ml_scr[rows, :] = ml
        z2 = mid + vecs["down_bias"]
        for f in range(FF // 256):
            cols = slice(256 * f, 256 * f + 256)
            up = dot(ml, up_w[:, cols]) + vecs["up_bias"][:, cols]
            act, slope = gelu_and_slope(up)
            act_scr[rows, cols] = act.astype(bf)
            slope_scr[:, cols] = slope
        z2 = z2 + dot(act_scr[rows, :], down_w[...])
        unit2, inv2 = normalized(z2)
        out_ref[rows, :] = (unit2 * vecs["ffn_gain"] + vecs["ffn_shift"]).astype(bf)
        dh = og_ref[rows, :].astype(f32)
        add_vector(dvec_ref, "ffn_gain", column_sum(dh * unit2))
        add_vector(dvec_ref, "ffn_shift", column_sum(dh))
        dz2 = norm_back(dh, vecs["ffn_gain"], unit2, inv2)
        ddown = dz2.astype(bf)
        ddown_scr[rows, :] = ddown
        add_vector(dvec_ref, "down_bias", column_sum(ddown.astype(f32)))
        for f in range(FF // 256):
            cols = slice(256 * f, 256 * f + 256)
            dup = (dot(ddown, down_w[cols, :], NT) * slope_scr[:, cols]).astype(bf)
            dup_scr[rows, cols] = dup
        add_vector(dvec_ref, "up_bias", column_sum(dup_scr[rows, :].astype(f32)))
        dmid = dz2 + dot(dup_scr[rows, :], up_w[...], NT)
        add_vector(dvec_ref, "attn_gain", column_sum(dmid * unit1))
        add_vector(dvec_ref, "attn_shift", column_sum(dmid))
        dz1 = norm_back(dmid, vecs["attn_gain"], unit1, inv1)
        dz1_ref[rows, :] = dz1
        dattn = dz1.astype(bf)
        dattn_scr[rows, :] = dattn
        add_vector(dvec_ref, "output_b", column_sum(dattn.astype(f32)))
        dctx = dot(dattn, output_w[...], NT).astype(bf)
        for p in range(PAIRS):
            dctx_ref[p, rows, :] = dctx[:, 128 * p : 128 * p + 128]
        return carry

    lax.fori_loop(0, tokens // C, chunk, 0)
    place = matrix_rows()

    def put(name, first, rows, value):
        base, _, pieces = place[name]
        for c in range(value.shape[1] // 128):
            wide[pl.ds(base - FEED_FIRST + pieces * first[0] + first[1] + c, rows, stride=pieces), :] = value[:, 128 * c : 128 * c + 128]

    ctx = jnp.concatenate([ctx_ref[p] for p in range(PAIRS)], axis=1)
    put("output_w", (0, 0), D, dot(ctx, dattn_scr[...], TN))
    for f in range(FF // 256):
        cols = slice(256 * f, 256 * f + 256)
        put("up_w", (0, 2 * f), D, dot(ml_scr[...], dup_scr[:, cols], TN))
        put("down_w", (256 * f, 0), 256, dot(act_scr[:, cols], ddown_scr[...], TN))


def split(values):
    high = values.astype(bf)
    return high, (values - high.astype(f32)).astype(bf)


def dot2(left, right, dims=NN):
    if left.dtype == f32:
        return sum(dot(part, right, dims) for part in split(left))
    return sum(dot(left, part, dims) for part in split(right))


def tail_local(dq_ref, x_ref, dz1_ref, query_w, dx_ref, dwq_ref, dvec_ref):
    tokens = dx_ref.shape[0]
    dq = jnp.concatenate([dq_ref[p] for p in range(PAIRS)], axis=1)
    dx_ref[...] = dz1_ref[...] + dot(dq, query_w[...], NT)
    dwq_ref[...] = dot(x_ref[SPAN : SPAN + tokens, :], dq, TN)
    put_vector(dvec_ref, "query_b", column_sum(dq.astype(f32)))


def tail_table(dkr_ref, dqr_ref, pos_ref, table_ref, vec_ref, query_w, key_w, dwq_ref, dwk_ref, dtable_ref, dvec_ref):
    JR = reversal()
    first = lax.broadcasted_iota(jnp.int32, (512, 384), 0) == 0
    dpos = None
    for ref, w, dw, name in ((dkr_ref, key_w, dwk_ref, "key_b"), (dqr_ref, query_w, dwq_ref, "query_b")):
        halves = jnp.concatenate([ref[p].T for p in range(PAIRS)], axis=1)
        tab = halves[:512] + jnp.where(first, column_sum(halves[512:]), 0.0)
        if name == "key_b":
            dw[...] = dot2(pos_ref[...], tab, TN)
            put_vector(dvec_ref, name, column_sum(tab))
        else:
            dw[...] += dot2(pos_ref[...], tab, TN)
            add_vector(dvec_ref, name, column_sum(tab))
        part = dot2(tab, w[...], NT)
        dpos = part if dpos is None else dpos + part
    unit, inverse = normalized(jnp.concatenate([dot(JR, table_ref[128 * b : 128 * b + 128, :]) for b in reversed(range(4))], axis=0))
    put_vector(dvec_ref, "rel_gain", column_sum(dpos * unit))
    put_vector(dvec_ref, "rel_shift", column_sum(dpos))
    dpos = norm_back(dpos, vector(vec_ref, "rel_gain"), unit, inverse).astype(bf)
    for b in range(4):
        dtable_ref[128 * b : 128 * b + 128, :] = dot(JR, dpos[128 * (3 - b) : 128 * (4 - b)])


def tail_keys(dk_ref, dv_ref, halo_ref, x_ref, key_w, value_w, dx_ref, dwk_ref, dwv_ref, dvec_ref):
    tokens = dx_ref.shape[0]
    x = x_ref[SPAN : SPAN + tokens, :]
    for which, (ref, w, dw, name) in enumerate(((dk_ref, key_w, dwk_ref, "key_b"), (dv_ref, value_w, dwv_ref, "value_b"))):
        pieces = []
        for p in range(PAIRS):
            own = ref[p, SPAN : SPAN + tokens, :]
            edge = [halo_ref[side, which, p].astype(f32) for side in (0, 1)]
            pieces.append(jnp.concatenate([own[:SPAN] + edge[0], own[SPAN : tokens - SPAN], own[tokens - SPAN :] + edge[1]], axis=0).astype(bf))
        d = jnp.concatenate(pieces, axis=1)
        dx_ref[...] += dot(d, w[...], NT)
        if name == "key_b":
            dw[...] += dot(x, d, TN)
            add_vector(dvec_ref, name, column_sum(d.astype(f32)))
        else:
            dw[...] = dot(x, d, TN)
            put_vector(dvec_ref, name, column_sum(d.astype(f32)))


def beside(grid, step):
    return {"seq": lax.axis_index("seq") + step, "row": lax.axis_index("row")}


def seq_edges(grid):
    s = lax.axis_index("seq")
    return s > 0, s < grid.seq - 1


def enter_all(grid, p):
    sem = pltpu.get_barrier_semaphore()
    total = jnp.int32(0)
    before, after = seq_edges(grid)
    targets = [(grid.device(q), cond) for _, q, cond in neighbours_of(grid, p)]
    targets += [(beside(grid, -1), before), (beside(grid, 1), after)]
    for device, cond in targets:
        guarded(cond, lambda device=device: pl.semaphore_signal(sem, inc=1, device_id=device, device_id_type=MESH))
        total = total + (1 if cond is None else cond.astype(jnp.int32))
    pl.semaphore_wait(sem, total)


def remote(source, target, send_sem, recv_sem, device):
    return pltpu.make_async_remote_copy(
        src_ref=source, dst_ref=target, send_sem=send_sem, recv_sem=recv_sem, device_id=device, device_id_type=MESH)


def assemble(grid, shard, slots, wide):
    for k in range(grid.count):
        low, high = shard * k // GROUP, -(-shard * (k + 1) // GROUP)
        shared = k + 1 < grid.count and shard * (k + 1) % GROUP != 0
        begin = low + (1 if k > 0 and shard * k % GROUP != 0 else 0)
        end = high - (1 if shared else 0)
        if end > begin:
            wide[16 * begin : 16 * end, :] = slots[k, 16 * (begin - low) : 16 * (end - low), :].astype(f32)
        if shared:
            wide[16 * end : 16 * high, :] = slots[k, 16 * (end - low) : 16 * (high - low), :].astype(f32) + slots[k + 1, 0:16, :].astype(f32)


def unpack(wide, outs, vec_ref):
    place = matrix_rows()
    for name, out in zip(MATRICES, outs):
        base, rows, pieces = place[name]
        for c in range(pieces):
            out[:, 128 * c : 128 * c + 128] = wide[pl.ds(base + c, rows, stride=pieces), :].astype(bf)
    vec_at, vec_total = vector_rows()
    vec_ref[...] = jnp.zeros((vec_total, 128), f32)
    for name in VECTORS:
        base, _, pieces = place[name]
        vec_ref[vec_at[name][0] : vec_at[name][0] + pieces, :] = wide[base : base + pieces, :]


def gather_kernel(grid, shard, slot_ref, x_ref, seg_ref, *refs):
    many = len(MATRICES)
    outs, (vec_ref, x_ext, seg_ext) = refs[:many], refs[many : many + 3]
    slots, wide, local_sem, send_sem, recv_sem, halo_send, halo_recv = refs[many + 3 :]
    p = grid.here()
    tokens = x_ref.shape[0]
    _, groups = shard_groups(shard, grid.count)
    before, after = seq_edges(grid)
    own = pltpu.make_async_copy(slot_ref, slots.at[grid.flat(p)], local_sem)
    own.start()
    enter_all(grid, p)
    own.wait()

    def halo_copies(side):
        step = -1 if side == 0 else 1
        take = pl.ds(0, SPAN) if side == 0 else pl.ds(tokens - SPAN, SPAN)
        land = pl.ds(tokens + SPAN, SPAN) if side == 0 else pl.ds(0, SPAN)
        return [
            remote(x_ref.at[take, :], x_ext.at[land, :], halo_send.at[side, 0], halo_recv.at[side, 0], beside(grid, step)),
            remote(seg_ref.at[:, take], seg_ext.at[:, land], halo_send.at[side, 1], halo_recv.at[side, 1], beside(grid, step)),
        ]

    def start(side):
        for copy in halo_copies(side):
            copy.start()

    pl.when(before)(lambda: start(0))
    pl.when(after)(lambda: start(1))

    def clear(rows):
        x_ext[rows, :] = jnp.zeros((SPAN, D), bf)
        seg_ext[:, rows] = jnp.zeros((8, SPAN), jnp.int32)

    pl.when(jnp.logical_not(before))(lambda: clear(pl.ds(0, SPAN)))
    pl.when(jnp.logical_not(after))(lambda: clear(pl.ds(tokens + SPAN, SPAN)))
    x_ext[SPAN : SPAN + tokens, :] = x_ref[...]
    seg_ext[:, SPAN : SPAN + tokens] = seg_ref[...]
    Gather(grid, p, slots, send_sem, recv_sem, groups).run()
    assemble(grid, shard, slots, wide)
    unpack(wide, outs, vec_ref)

    def end(side):
        for copy in halo_copies(side):
            copy.wait_send()

    def landed(side):
        for copy in halo_copies(side):
            copy.wait_recv()

    pl.when(before)(lambda: end(0))
    pl.when(after)(lambda: end(1))
    pl.when(after)(lambda: landed(0))
    pl.when(before)(lambda: landed(1))


VMEM = pl.BlockSpec(memory_space=pltpu.VMEM)


def matrix_shapes(dtype):
    return [jax.ShapeDtypeStruct((matrix_rows()[name][1], 128 * matrix_rows()[name][2]), dtype) for name in MATRICES]


def gather_params(grid, shard, slot, x, seg):
    _, groups = shard_groups(shard, grid.count)
    tokens = x.shape[0]
    total = flat_rows(shard, grid.count)
    return pl.pallas_call(
        functools.partial(gather_kernel, grid, shard),
        out_shape=matrix_shapes(bf)
        + [
            jax.ShapeDtypeStruct((vector_rows()[1], 128), f32),
            jax.ShapeDtypeStruct((tokens + 2 * SPAN, D), bf),
            jax.ShapeDtypeStruct((8, tokens + 2 * SPAN), jnp.int32),
        ],
        in_specs=[VMEM] * 3,
        out_specs=[VMEM] * (len(MATRICES) + 3),
        scratch_shapes=[
            pltpu.VMEM((grid.count, 16 * groups, 128), bf),
            pltpu.VMEM((total, 128), f32),
            pltpu.SemaphoreType.DMA,
            pltpu.SemaphoreType.DMA((count_sends(grid, groups),)),
            pltpu.SemaphoreType.DMA((len(orders_of(groups)), grid.count)),
            pltpu.SemaphoreType.DMA((2, 2)),
            pltpu.SemaphoreType.DMA((2, 2)),
        ],
        compiler_params=pltpu.CompilerParams(collective_id=0, has_side_effects=True, vmem_limit_bytes=48 << 20),
    )(slot, x, seg)


def forward_kernel(x_ref, seg_ref, query_w, key_w, value_w, table_ref, vec_ref, q_ref, k_ref, v_ref, krt_ref, qrt_ref, pos_ref, ctx_ref, p_ref, x_scr, bias_scr):
    project_body(x_ref, query_w, key_w, value_w, table_ref, vec_ref, q_ref, k_ref, v_ref, krt_ref, qrt_ref, pos_ref)
    att_fwd_body(q_ref.shape[1] // 128, q_ref, k_ref, v_ref, krt_ref, qrt_ref, seg_ref, ctx_ref, p_ref, x_scr, bias_scr)


def forward(x_ext, seg_ext, query_w, key_w, value_w, table, vec):
    E = x_ext.shape[0]
    T = E - 2 * SPAN
    blocks = T // 128
    shape = jax.ShapeDtypeStruct
    return pl.pallas_call(
        forward_kernel,
        out_shape=[
            shape((PAIRS, T, 128), bf), shape((PAIRS, E, 128), bf), shape((PAIRS, E, 128), bf), shape((PAIRS, 640, 128), bf),
            shape((PAIRS, 640, 128), bf), shape((512, D), bf), shape((PAIRS, T, 128), bf), shape((PAIRS, blocks, 2, 128, 640), bf),
        ],
        in_specs=[VMEM] * 7,
        out_specs=[VMEM] * 8,
        scratch_shapes=[pltpu.VMEM((2, blocks + 5, 128, 640), bf), pltpu.VMEM((blocks, 128, 640), f32)],
        compiler_params=pltpu.CompilerParams(vmem_limit_bytes=56 << 20),
    )(x_ext, seg_ext, query_w, key_w, value_w, table, vec)


def feed_kernel(x_ref, ctx_ref, og_ref, output_w, up_w, down_w, vec_ref, out_ref, dz1_ref, dctx_ref, dflat_ref, dvec_ref, ml, dup, act, ddown, dattn, slope, wide):
    feed_body(x_ref, ctx_ref, og_ref, output_w, up_w, down_w, vec_ref, out_ref, dz1_ref, dctx_ref, wide, dvec_ref, ml, dup, act, ddown, dattn, slope)
    dflat_ref[...] = wide[...].astype(bf)


def feed(x_ext, ctx, out_grad, output_w, up_w, down_w, vec):
    T = out_grad.shape[0]
    shape = jax.ShapeDtypeStruct
    return pl.pallas_call(
        feed_kernel,
        out_shape=[shape((T, D), bf), shape((T, D), f32), shape((PAIRS, T, 128), bf), shape((FEED_ROWS, 128), bf), shape(vec.shape, f32)],
        in_specs=[VMEM] * 7,
        out_specs=[VMEM] * 5,
        scratch_shapes=[
            pltpu.VMEM((T, D), bf), pltpu.VMEM((T, FF), bf), pltpu.VMEM((T, FF), bf), pltpu.VMEM((T, D), bf), pltpu.VMEM((T, D), bf),
            pltpu.VMEM((256, FF), f32), pltpu.VMEM((FEED_ROWS, 128), f32),
        ],
        compiler_params=pltpu.CompilerParams(vmem_limit_bytes=56 << 20),
    )(x_ext, ctx, out_grad, output_w, up_w, down_w, vec)


def tail_kernel(grid, shard, dq_ref, dk_ref, dv_ref, dkr_ref, dqr_ref, dz1_ref, x_ref, pos_ref, table_ref, vec_ref, query_w, key_w, value_w, dflat_ref, dvec_in,
                dx_ref, sum_ref, dvec_ref, dwq, dwk, dwv, dtable, wide, flat, kids, outgoing, total, halo_out, halo_in, send_sem, recv_sem, halo_send, halo_recv):
    p = grid.here()
    tokens = dx_ref.shape[0]
    _, groups = shard_groups(shard, grid.count)
    before, after = seq_edges(grid)
    enter_all(grid, p)
    rims = (pl.ds(0, SPAN), pl.ds(tokens + SPAN, SPAN))
    for side in (0, 1):
        for which, ref in ((0, dk_ref), (1, dv_ref)):
            halo_out[side, which] = ref[:, rims[side], :].astype(bf)

    def halo_copy(side):
        return remote(halo_out.at[side], halo_in.at[1 - side], halo_send.at[side], halo_recv.at[1 - side], beside(grid, -1 if side == 0 else 1))

    pl.when(before)(lambda: halo_copy(0).start())
    pl.when(after)(lambda: halo_copy(1).start())

    def clear(side):
        halo_in[side] = jnp.zeros(halo_in.shape[1:], bf)

    pl.when(jnp.logical_not(before))(lambda: clear(0))
    pl.when(jnp.logical_not(after))(lambda: clear(1))
    dvec_ref[...] = dvec_in[...]
    tail_local(dq_ref, x_ref, dz1_ref, query_w, dx_ref, dwq, dvec_ref)
    tail_table(dkr_ref, dqr_ref, pos_ref, table_ref, vec_ref, query_w, key_w, dwq, dwk, dtable, dvec_ref)
    pl.when(before)(lambda: halo_copy(0).wait_send())
    pl.when(after)(lambda: halo_copy(1).wait_send())
    pl.when(before)(lambda: halo_copy(1).wait_recv())
    pl.when(after)(lambda: halo_copy(0).wait_recv())
    tail_keys(dk_ref, dv_ref, halo_in, x_ref, key_w, value_w, dx_ref, dwk, dwv, dvec_ref)
    place = matrix_rows()
    rest = flat.shape[0] - FEED_FIRST - FEED_ROWS
    wide[FEED_FIRST:, :] = jnp.zeros((rest, 128), f32)
    moved = lambda row: row if row < FEED_FIRST else row - FEED_ROWS
    for name, ref in (("query_w", dwq), ("key_w", dwk), ("value_w", dwv), ("rel_table", dtable)):
        base, rows, pieces = place[name]
        for c in range(pieces):
            wide[pl.ds(moved(base) + c, rows, stride=pieces), :] = ref[:, 128 * c : 128 * c + 128]
    vec_at, _ = vector_rows()
    for name in VECTORS:
        base, _, pieces = place[name]
        wide[moved(base) : moved(base) + pieces, :] = dvec_ref[vec_at[name][0] : vec_at[name][0] + pieces, :]
    flat[0:FEED_FIRST, :] = wide[0:FEED_FIRST, :].astype(bf)
    flat[FEED_FIRST : FEED_FIRST + FEED_ROWS, :] = dflat_ref[...]
    flat[FEED_FIRST + FEED_ROWS :, :] = wide[FEED_FIRST:, :].astype(bf)
    Scatter(grid, p, flat, lambda k: (k * shard // GROUP) * 16, kids, outgoing, total, send_sem, recv_sem, groups).run(sum_ref)


def tail(grid, shard, *args):
    _, groups = shard_groups(shard, grid.count)
    rows = flat_rows(shard, grid.count)
    tokens = args[5].shape[0]
    names, half = len(direction_names(grid)), grid.count // 2
    shape = jax.ShapeDtypeStruct
    dx, summed, _ = pl.pallas_call(
        functools.partial(tail_kernel, grid, shard),
        out_shape=[shape((tokens, D), f32), shape((16 * groups, 128), f32), shape((vector_rows()[1], 128), f32)],
        in_specs=[VMEM] * 15,
        out_specs=[VMEM] * 3,
        scratch_shapes=[
            pltpu.VMEM((D, D), f32), pltpu.VMEM((D, D), f32), pltpu.VMEM((D, D), f32), pltpu.VMEM((2 * SPAN, D), f32),
            pltpu.VMEM((rows - FEED_ROWS, 128), f32),
            pltpu.VMEM((rows, 128), bf),
            pltpu.VMEM((names, half, 16 * groups, 128), bf),
            pltpu.VMEM((half, 16 * groups, 128), bf),
            pltpu.VMEM((16 * groups, 128), f32),
            pltpu.VMEM((2, 2, PAIRS, SPAN, 128), bf),
            pltpu.VMEM((2, 2, PAIRS, SPAN, 128), bf),
            pltpu.SemaphoreType.DMA((scatter_sends(grid, groups),)),
            pltpu.SemaphoreType.DMA((len(orders_of(groups)), names, half)),
            pltpu.SemaphoreType.DMA((2,)),
            pltpu.SemaphoreType.DMA((2,)),
        ],
        compiler_params=pltpu.CompilerParams(collective_id=1, has_side_effects=True, vmem_limit_bytes=60 << 20),
    )(*args)
    return dx, summed


def on_device(layer_input, segment_ids, out_grad, weights, momentum, average):
    tokens_here = layer_input.shape[1]
    grid = Grid(lax.axis_size("seq"), lax.axis_size("row"))
    shard = weights.shape[0]
    _, groups = shard_groups(shard, grid.count)
    shift = (lax.axis_index("seq") * grid.row + lax.axis_index("row")) * shard % GROUP
    slot = lax.dynamic_update_slice(jnp.zeros((GROUP * groups,), bf), weights.astype(bf), (shift,)).reshape(16 * groups, 128)
    seg = jnp.broadcast_to(segment_ids + 1, (8, tokens_here))
    *matrices, vec, x_ext, seg_ext = gather_params(grid, shard, slot, layer_input[0], seg)
    query_w, key_w, value_w, output_w, up_w, down_w, table = matrices
    q, k, v, krt, qrt, pos, ctx, probs = forward(x_ext, seg_ext, query_w, key_w, value_w, table, vec)
    block_output, dz1, dctx, dflat, dvec = feed(x_ext, ctx, out_grad[0], output_w, up_w, down_w, vec)
    dq, dk, dv, dkr, dqr = att_bwd(q, k, v, krt, qrt, dctx, probs)
    dx, summed = tail(grid, shard, dq, dk, dv, dkr, dqr, dz1, x_ext, pos, table, vec, query_w, key_w, value_w, dflat, dvec)
    weight_grad = lax.dynamic_slice(summed.reshape(-1), (shift,), (shard,))
    all_tokens = tokens_here * grid.seq * layer_input.shape[0] * grid.row
    rate = 0.1 / math.sqrt(all_tokens)
    new_momentum = 0.5 * momentum + weight_grad
    new_weights = weights - rate * (weight_grad + 0.5 * new_momentum)
    new_average = 0.5 * average + 0.5 * new_weights
    return (
        block_output[None],
        dx[None],
        weight_grad,
        new_momentum,
        new_average,
        new_weights,
        new_weights.astype(jnp.bfloat16),
    )


def solution(mesh):
    flat = P(("seq", "row"))
    tokens = P("row", "seq", None)
    return jax.shard_map(
        on_device,
        mesh=mesh,
        in_specs=(tokens, P("row", "seq"), tokens, flat, flat, flat),
        out_specs=(tokens, tokens, flat, flat, flat, flat, flat),
        check_vma=False,
    )
```

profile of v0, /device:TPU:0, one launch (start us, length us, event | category | flops | bytes accessed | tf_op | source)
XLA Modules:
  0.0 236.9 jit_solution(6550917755085786041)
XLA Ops:
  0.7 0.7 broadcast_add_fusion
  1.4 1.0 convert_element_type.6
  2.3 1.2 dynamic_update_slice.3
  3.5 0.0 copy-start.12
  3.6 1.1 copy-done.12
  4.7 34.9 %shard_map.117 = (bf16[384,384]{1,0:T(8,128)(2,1)S(1)}, bf16[384,384]{1,0:T(8,128)(2,1)S(1)}, bf16[384,384]{1,0:T(8,128)(2,1)S(1)}, bf16[384,384]{1,0:T(8,128)(2...) custom-call(bf16[512,128]{1,0:T(8,128)(2,1)S(1)} %bitcast.8, ...), custom_call_target="tpu_custom_call" | custom-call | tf_op jit(solution)/shard_map/pallas_call | solution.py:852
  39.6 0.0 copy-start
  39.6 1.0 copy-done
  40.6 0.0 copy-start.1
  40.6 0.8 copy-done.1
  41.4 0.0 copy-start.2
  41.4 1.0 copy-done.2
  42.4 0.0 copy-start.3
  42.4 1.1 copy-done.3
  43.5 0.0 copy-start.4
  43.5 0.7 copy-done.4
  44.2 0.0 copy-start.5
  44.2 0.7 copy-done.5
  44.9 0.0 copy-start.6
  44.9 0.7 copy-done.6
  45.7 0.0 copy-start.15
  45.7 0.7 copy-done.15
  46.4 0.0 copy-start.16
  46.4 0.6 copy-done.16
  47.0 0.0 copy-start.17
  47.0 0.6 copy-done.17
  47.6 48.9 %shard_map.118 = (bf16[3,1024,128]{2,1,0:T(8,128)(2,1)}, bf16[3,1536,128]{2,1,0:T(8,128)(2,1)}, bf16[3,1536,128]{2,1,0:T(8,128)(2,1)}, bf16[3,640,128]{2,1,0:T(8...) custom-call(bf16[1536,384]{1,0:T(8,128)(2,1)} %copy-done, ...), custom_call_target="tpu_custom_call" | custom-call | tf_op jit(solution)/shard_map/pallas_call | solution.py:885
  96.5 0.0 copy-start.14
  96.5 20.3 %shard_map.119 = (bf16[1024,384]{1,0:T(8,128)(2,1)}, f32[1024,384]{1,0:T(8,128)}, bf16[3,1024,128]{2,1,0:T(8,128)(2,1)}, bf16[10368,128]{1,0:T(8,128)(2,1)}, f32[48,128]{1,0:T(8,128)}) custom-call(bf16[1536,384]{1,0:T(8,128)(2,1)} %copy-done, bf16[3,1024,128]{2,1,0:T(8,128)(2,1)} %get-tuple-element.44.ctx_ref, bf16[1024,384]{1,0:T(8,128)(2,1)} %bitcast.10, ...), custom_call_target="tpu_custom_call" | custom-call | tf_op jit(solution)/shard_map/pallas_call | solution.py:906
  116.8 0.0 copy-done.10
  116.9 0.0 copy-done.13
  116.9 0.0 copy-done.14
  116.9 0.0 copy-start.11
  116.9 1.1 copy-done.11
  118.0 66.3 %shard_map.120 = (bf16[3,1024,128]{2,1,0:T(8,128)(2,1)S(1)}, f32[3,1536,128]{2,1,0:T(8,128)}, f32[3,1536,128]{2,1,0:T(8,128)}, f32[3,128,640]{2,1,0:T(8,128)S(1)}, f32[3,128,640]{2,1,0:T(8,128)S(1)}) custom-call(bf16[3,1024,128]{2,1,0:T(8,128)(2,1)S(1)} %copy-done.10, bf16[3,1536,128]{2,1,0:T(8,128)(2,1)} %get-tuple-element.50.k_ref, ...), custom_call_target="tpu_custom_call" | custom-call | tf_op jit(solution)/shard_map/pallas_call | solution.py:509
  184.3 1.0 copy-done.7
  185.2 0.9 copy-done.8
  186.2 0.9 copy-done.9
  187.1 45.8 %shard_map.121 = (f32[1024,384]{1,0:T(8,128)}, f32[512,128]{1,0:T(8,128)}, f32[48,128]{1,0:T(8,128)}) custom-call(bf16[3,1024,128]{2,1,0:T(8,128)(2,1)} %copy-done.9, f32[3,1536,128]{2,1,0:T(8,128)} %get-tuple-element.57.dk_ref, f32[3,1536,128]{2,1,0:T(8,128)} %get-tuple-element.58.dv_ref, f32[3,128,640]{2,1,0:T(8,128)} %copy-done.7, ...), custom_call_target="tpu_custom_call" | custom-call | tf_op jit(solution)/shard_map/pallas_call | solution.py:974
  232.9 0.0 copy-start.18
  232.9 0.0 copy-done.19
  232.9 0.0 copy-done.21
  232.9 2.0 fusion
  234.9 0.0 copy-done.22
  234.9 0.8 add_multiply_fusion
  235.7 0.0 copy-done.18
  235.7 1.1 copy.15
  236.8 0.0 copy-done.20
  (11 shorter events, 0.0 us)
Async XLA Ops:
  3.5 1.1 copy-start.12
  39.6 1.0 copy-start
  40.6 0.8 copy-start.1
  41.4 1.0 copy-start.2
  42.4 1.1 copy-start.3
  43.5 0.7 copy-start.4
  44.2 0.7 copy-start.5
  44.9 0.7 copy-start.6
  45.7 0.7 copy-start.15
  46.4 0.6 copy-start.16
  47.0 0.6 copy-start.17
  96.5 20.3 %copy-start.10 = (bf16[3,1024,128]{2,1,0:T(8,128)(2,1)S(1)}, bf16[3,1024,128]{2,1,0:T(8,128)(2,1)}, u32[]{:S(2)}) copy-start(bf16[3,1024,128]{2,1,0:T(8,128)(2,1)} %get-tuple-element.49.q_ref) | copy-start | bytes 2359300
  96.5 20.3 %copy-start.13 = (bf16[3,640,128]{2,1,0:T(8,128)(2,1)S(1)}, bf16[3,640,128]{2,1,0:T(8,128)(2,1)}, u32[]{:S(2)}) copy-start(bf16[3,640,128]{2,1,0:T(8,128)(2,1)} %get-tuple-element.52.krt_ref) | copy-start | bytes 1474564
  96.5 20.4 %copy-start.14 = (bf16[3,640,128]{2,1,0:T(8,128)(2,1)S(1)}, bf16[3,640,128]{2,1,0:T(8,128)(2,1)}, u32[]{:S(2)}) copy-start(bf16[3,640,128]{2,1,0:T(8,128)(2,1)} %get-tuple-element.53.qrt_ref) | copy-start | bytes 1474564
  116.9 1.1 copy-start.11
  184.3 1.0 copy-start.7
  185.2 1.0 copy-start.8
  186.2 0.9 copy-start.9
  187.1 45.8 %copy-start.19 = (f32[61620]{0:T(1024)S(1)}, f32[61620]{0:T(1024)}, u32[]{:S(2)}) copy-start(f32[61620]{0:T(1024)} %param.9) | copy-start | bytes 739444
  187.1 45.8 %copy-start.21 = (f32[61620]{0:T(1024)S(1)}, f32[61620]{0:T(1024)}, u32[]{:S(2)}) copy-start(f32[61620]{0:T(1024)} %param.10) | copy-start | bytes 739444
  187.1 47.9 %copy-start.22 = (f32[61620]{0:T(1024)S(1)}, f32[61620]{0:T(1024)}, u32[]{:S(2)}) copy-start(f32[61620]{0:T(1024)} %param.11) | copy-start | bytes 739444
  232.9 2.8 %copy-start.18 = (f32[1024,384]{1,0:T(8,128)S(1)}, f32[1024,384]{1,0:T(8,128)}, u32[]{:S(2)}) copy-start(f32[1024,384]{1,0:T(8,128)} %get-tuple-element.65) | copy-start | bytes 4718596
  234.9 1.9 copy-start.20
where the time goes:
time: 237 us
  Pallas kernels  216 us (91%)
  local copies, waits for them, and re-layouts  15.4 us (6%)
  other arithmetic  4.45 us (2%)
    pallas_call x1, Pallas kernels, att_bwd(): pl.pallas_call(functools.partial(att_bwd_body, nblk), out_shape=[jax.Shap...  66.3 us
    pallas_call x1, Pallas kernels, forward(): pl.pallas_call(forward_kernel, out_shape=[shape((PAIRS, T, 128), bf), sha...  48.9 us
    pallas_call x1, Pallas kernels, tail(): pl.pallas_call(functools.partial(tail_kernel, grid, shard), out_shape=[sh...  45.8 us
    pallas_call x1, Pallas kernels, gather_params(): pl.pallas_call(functools.partial(gather_kernel, grid, shard), out_shape=m...  34.9 us
    pallas_call x1, Pallas kernels, feed(): pl.pallas_call(feed_kernel, out_shape=[shape((T, D), bf), shape((T, D), f...  20.3 us
    unnamed x47, local copies, waits for them, and re-layouts  14.2 us

commit v1 on v0

--- a/solution.py
+++ b/solution.py
@@ -359,159 +359,314 @@
     return place, -(-at // 8) * 8
 
 
-SC = 1.0/math.sqrt(3.0*HEAD_DIM)
+SC = 1.0 / math.sqrt(3.0 * HEAD_DIM)
 LOG2E = 1.4426950408889634
-NT=(((1,),(1,)),((),())); NN=(((1,),(0,)),((),())); TN=(((0,),(0,)),((),()))
-def dot(a,b,d=NN): return lax.dot_general(a,b,d,preferred_element_type=f32)
-
-def head_mask(rows, h):
-    lane=lax.broadcasted_iota(jnp.int32,(rows,128),1)
-    return (lane<64) if h==0 else (lane>=64)
-def keep(x,h):
-    return jnp.where(head_mask(x.shape[0],h), x, jnp.zeros_like(x))
-
-def skew(A):
-    return jnp.concatenate([pltpu.roll(A[8*g:8*g+8,:512],8*g+1,1,stride=1,stride_axis=0) for g in range(16)],axis=0)
-
-
-def att_fwd_body(nblk, q_ref,k_ref,v_ref,krt_ref,qrt_ref,seg_ref,ctx_ref,p_ref,x_scr,bias_scr):
-    row=lax.broadcasted_iota(jnp.int32,(128,128),0); lane=lax.broadcasted_iota(jnp.int32,(128,128),1)
-    eye=(row==lane).astype(bf)
-    def mk_bias(t,c):
-        off=pl.multiple_of(t*128,128)
-        sq=jnp.broadcast_to(seg_ref[0:1,pl.ds(pl.multiple_of(off+SPAN,128),128)],(128,128)).astype(f32).T
+NT = (((1,), (1,)), ((), ()))
+NN = (((1,), (0,)), ((), ()))
+TN = (((0,), (0,)), ((), ()))
+
+
+def dot(a, b, dims=NN):
+    return lax.dot_general(a, b, dims, preferred_element_type=f32)
+
+
+def iotas(rows, lanes):
+    return lax.broadcasted_iota(jnp.int32, (rows, lanes), 0), lax.broadcasted_iota(jnp.int32, (rows, lanes), 1)
+
+
+def tile(i):
+    return pl.ds(pl.multiple_of(i * 128, 128), 128)
+
+
+def window(i):
+    return pl.ds(pl.multiple_of(i * 128, 128), NB * 128)
+
+
+def wide_diagonal(columns):
+    zero = jnp.zeros((64, 128), columns.dtype)
+    return jnp.concatenate([jnp.concatenate([columns[:64], zero], axis=1), jnp.concatenate([zero, columns[64:]], axis=1)], axis=0)
+
+
+def tall_diagonal(rows):
+    lane = iotas(128, 128)[1]
+    zero = jnp.zeros_like(rows)
+    return jnp.concatenate([jnp.where(lane < 64, rows, zero), jnp.where(lane >= 64, rows, zero)], axis=0)
+
+
+def own_heads(wide):
+    return jnp.concatenate([wide[:64, :128], wide[64:, 128:]], axis=0)
+
+
+def turn_rows(values, back):
+    size = values.shape[0]
+    lane = iotas(*values.shape)[1]
+    for step in (64, 32, 16, 8, 4, 2, 1):
+        moved = pltpu.roll(values, size - step if back else step, 0)
+        values = jnp.where(lane & step != 0, moved, values)
+    return values
+
+
+def turn_lanes(values, first):
+    return jnp.concatenate([pltpu.roll(values[8 * g : 8 * g + 8, :512], first + 8 * g, 1, stride=1, stride_axis=0) for g in range(16)], axis=0)
+
+
+def stream_rows(load, up, fine):
+    row, lane = iotas(8, 128)
+    inner = [(step, lane & step != 0, row < step if not up else row >= 8 - step) for step in fine]
+    masks = [lane & step != 0 for step in (8, 16, 32, 64)]
+    turned = [None for _ in inner]
+    past = [[] for _ in masks]
+    extra = 15 + len(inner)
+    order = list(range(64 - extra, 64)) + list(range(64)) if not up else list(reversed(list(range(64)) + list(range(extra))))
+    for n, i in enumerate(order):
+        value = load(i)
+        for level, (step, mask, edge) in enumerate(inner):
+            now = pltpu.roll(value, step if not up else 8 - step, 0)
+            if turned[level] is not None:
+                value = jnp.where(mask, jnp.where(edge, turned[level], now), value)
+            turned[level] = now
+        for level, mask in enumerate(masks):
+            past[level].append(value)
+            if len(past[level]) > 1 << level:
+                value = jnp.where(mask, past[level].pop(0), value)
+        if n >= extra:
+            yield i, value
+
+
+def att_fwd_body(nblk, qT_ref, k_ref, vT_ref, krt_ref, qrtT_ref, seg_ref, ctx_ref, p_ref, inv_ref, x_scr, bias_scr, s0, s1, z0, z1, t0, t1, m0, m1):
+    row, lane = iotas(128, 128)
+    lane2 = iotas(128, 256)[1]
+    lane512 = iotas(512, 256)[1]
+    items, keys = PAIRS * nblk, nblk + 4
+
+    def mk_bias(t, carry):
+        sq = seg_ref[0:1, tile(t + 2)].astype(f32)
         for b in range(NB):
-            sk=seg_ref[0:1,pl.ds(pl.multiple_of(off+128*b,128),128)].astype(f32)
-            ok = sq==sk
-            if b==0: ok = ok & (lane>=row)
-            if b==NB-1: ok = ok & (lane<=row)
-            bias_scr[t,:,128*b:128*b+128]=jnp.where(ok,0.0,-1e30).astype(f32)
-        return c
-    lax.fori_loop(0,nblk,mk_bias,0)
-    def pair(p,c):
-        def keyside(J):
-            kj=k_ref[p,pl.ds(pl.multiple_of(jnp.minimum(J,nblk+3)*128,128),128),:]
+            sk = jnp.broadcast_to(seg_ref[0:1, tile(t + b)], (128, 128)).astype(f32).T
+            ok = sk == sq
+            if b == 0:
+                ok = ok & (row >= lane)
+            if b == NB - 1:
+                ok = ok & (row <= lane)
+            bias_scr[t, 128 * b : 128 * b + 128, :] = jnp.where(ok, 0.0, -1e30).astype(f32)
+        return carry
+
+    lax.fori_loop(0, nblk, mk_bias, 0)
+
+    def keyside(p, J, slot):
+        C = dot(tall_diagonal(k_ref[p, tile(J), :]), qrtT_ref[p])
+        for h in range(2):
+            Ch = C[128 * h : 128 * h + 128]
+            R = turn_lanes(Ch, 0)
+            x_scr[slot, h, :, 0:128] = jnp.where(lane > row, R[:, :128], Ch[:, 512:]).astype(bf)
+            x_scr[slot, h, :, 128:512] = R[:, 128:].astype(bf)
+            x_scr[slot, h, :, 512:640] = R[:, :128].astype(bf)
+
+    def start(J, carry):
+        keyside(0, J, J)
+        return carry
+
+    lax.fori_loop(0, keys, start, 0)
+
+    def scores(n, s_scr, z_scr, t_scr, m_scr):
+        n = jnp.minimum(n, items - 1)
+        p, t = n // nblk, n % nblk
+        base = (p % 2) * keys + t
+        Q2 = wide_diagonal(qT_ref[p, :, tile(t)])
+        odd = lane2 % 2 == 1
+        zero = jnp.zeros_like(Q2)
+        table = krt_ref[p]
+        moved = krt_ref[PAIRS + p]
+        Z = dot(jnp.concatenate([table, moved], axis=1), jnp.concatenate([jnp.where(odd, zero, Q2), jnp.where(odd, Q2, zero)], axis=0))
+        ends = jnp.where(odd[:1], Z[2:3], Z[1:2])
+        z_scr[...] = Z
+        s_scr[...] = dot(k_ref[p, window(t), :], Q2)
+        for h in range(2):
+            cols = slice(128 * h, 128 * h + 128)
+
+            def load(i):
+                return z_scr[8 * i : 8 * i + 8, cols]
+
+            end = ends[:, cols]
+            top = None
+            held = None
+            for i, y in stream_rows(load, False, (2, 4)):
+                if i % 2 == 0:
+                    held = y
+                    continue
+                at, b = 8 * (i - 1), i // 16
+                y = jnp.concatenate([held, y], axis=0)
+                for block in (0, 4) if b == 0 else (b,):
+                    r = at + 128 * (block - b)
+                    rows = slice(r, r + 16)
+                    inner = slice(at % 128, at % 128 + 16)
+                    x = x_scr[base + block, h, inner, 128 * (4 - block) : 128 * (5 - block)].astype(f32)
+                    part = y
+                    if block == 0:
+                        part = jnp.where(iotas(16, 128)[0] + at > iotas(16, 128)[1], y, end)
+                    T = s_scr[rows, cols] + bias_scr[t, rows, :] + part + x
+                    t_scr[rows, cols] = T
+                    most = jnp.maximum(T[:8], T[8:])
+                    top = most if top is None else jnp.maximum(top, most)
+            m_scr[:, cols] = top
+
+    def soft(n, t_scr, m_scr):
+        n = jnp.clip(n, 0, items - 1)
+        m = jnp.max(m_scr[...], axis=0, keepdims=True)
+        total = None
+        for i in range(40):
+            e = jnp.exp2((t_scr[16 * i : 16 * i + 16, :] - m) * (SC * LOG2E))
+            part = e[:8] + e[8:]
+            total = part if total is None else total + part
+            p_ref[n // nblk, n % nblk, 16 * i : 16 * i + 16, :] = e.astype(bf)
+        inv_ref[n // nblk, n % nblk] = jnp.broadcast_to(1.0 / jnp.sum(total, axis=0, keepdims=True), (8, 256))
+
+    def context(n):
+        n = jnp.clip(n, 0, items - 1)
+        p, t = n // nblk, n % nblk
+        ctxT = own_heads(dot(vT_ref[p, :, window(t)], p_ref[p, t]) * inv_ref[p, t, 0:1, :])
+        ctx_ref[p, tile(t), :] = ctxT.astype(bf).T
+
+    half = nblk // 2
+    per = keys // half
+
+    def body(m, slot):
+        context(2 * m - 2)
+        soft(2 * m - 1, t1, m1)
+        scores(2 * m, s0, z0, t0, m0)
+        context(2 * m - 1)
+        soft(2 * m, t0, m0)
+        scores(2 * m + 1, s1, z1, t1, m1)
+        p, first = jnp.minimum(m // half + 1, PAIRS - 1), per * (m % half)
+        for i in range(per):
+            keyside(p, first + i, slot + i)
+        return jnp.where(slot + per == 2 * keys, 0, slot + per)
+
+    lax.fori_loop(0, items // 2 + 1, body, jnp.int32(keys))
+
+
+def unreversed(values, JR):
+    high = values.astype(bf)
+    low = (values - high.astype(f32)).astype(bf)
+    both = dot(JR, jnp.concatenate([high, low], axis=1))
+    return both[:, :128] + both[:, 128:]
+
+
+def att_bwd_body(nblk, q_ref, kT_ref, kTr_ref, v_ref, krtT_ref, qrt_ref, qend_ref, dctxT_ref, p_ref, inv_ref, dq_ref, dkc_ref, dkp_ref, dv_ref, dkr_ref, dqr_ref,
+                 gt_scr, dp_scr, gm_scr, gb0, gb1, gu0, gu1):
+    row, lane = iotas(128, 128)
+    row16, lane16 = iotas(16, 256)
+    JR = (row + lane == 127).astype(bf)
+    zero = jnp.zeros((128, 128), bf)
+    items, keys, half = PAIRS * nblk, nblk + 4, nblk // 2
+    per = keys // half
+    gt_scr[...] = jnp.zeros(gt_scr.shape, bf)
+    gb1[...] = jnp.zeros(gb1.shape, bf)
+    gu1[...] = jnp.zeros(gu1.shape, bf)
+    for ref in (dkc_ref, dv_ref, dkr_ref, dqr_ref):
+        ref[...] = jnp.zeros(ref.shape, f32)
+
+    def kblocks(p, first, base):
+        turned = [[], []]
+        for i in range(per):
             for h in range(2):
-                C=dot(keep(kj,h),qrt_ref[p],NT)
-                R=skew(C)
-                x_scr[h,J,:,0:128]=jnp.where(lane>row,R[:,:128],C[:,512:]).astype(bf)
-                x_scr[h,J,:,128:512]=R[:,128:].astype(bf)
-                x_scr[h,J,:,512:640]=R[:,:128].astype(bf)
-        def st(J,c):
-            keyside(J); return c
-        lax.fori_loop(0,5,st,0)
-        def qblock(t,c):
-            off=pl.multiple_of(t*128,128)
-            qt=q_ref[p,pl.ds(off,128),:]
-            kw=[k_ref[p,pl.ds(pl.multiple_of(off+128*b,128),128),:] for b in range(NB)]
-            vw=v_ref[p,pl.ds(off,640),:]
-            ctx=[]
+                GT = gt_scr[base + first + i, h]
+                Gm = jnp.concatenate([jnp.where(lane > row, GT[:, :128], GT[:, 512:]), GT[:, 128:512]], axis=1)
+                turned[h].append(turn_lanes(dot(JR, Gm), 385).astype(bf))
+        stacked = [jnp.concatenate(part, axis=0) for part in turned]
+        dk = dot(jnp.concatenate(stacked, axis=1), qrt_ref[p])
+        for i in range(per):
+            dkp_ref[p, tile(first + i), :] = unreversed(dk[128 * i : 128 * i + 128], JR)
+        span = pl.ds(pl.multiple_of(first * 128, 128), 128 * per)
+        for h in range(2):
+            heads = slice(64 * h, 64 * h + 64)
+            dqr_ref[p, heads, 0:512] += dot(kTr_ref[p, heads, span], stacked[h])
+
+    def upstream(n, slot, gb, gu):
+        p, t = n // nblk, n % nblk
+        D2 = wide_diagonal(dctxT_ref[p, :, tile(t)])
+        inv = inv_ref[p, t, 0:1, :]
+        dp_scr[...] = dot(v_ref[p, window(t), :], D2)
+        total = None
+        for i in range(40):
+            rows = slice(16 * i, 16 * i + 16)
+            w = p_ref[p, t, rows, :].astype(f32) * dp_scr[rows, :]
+            part = w[:8] + w[8:]
+            total = part if total is None else total + part
+        less = jnp.sum(total, axis=0, keepdims=True) * inv * inv
+
+        def grad(i):
+            rows = slice(16 * i, 16 * i + 16)
+            G = p_ref[p, t, rows, :].astype(f32) * (dp_scr[rows, :] * inv - less)
+            Gb = G.astype(bf)
+            gb[rows, :] = Gb
+            b = i // 8
             for h in range(2):
-                qm=keep(qt,h)
-                A=dot(qm,krt_ref[p],NT)
-                R=skew(A)
-                lhs=jnp.concatenate([qm,eye],axis=1)
-                rhs=jnp.concatenate([jnp.concatenate([kw[b],x_scr[h,t+b,:,128*(4-b):128*(5-b)]],axis=1) for b in range(NB)],axis=0)
-                S=dot(lhs,rhs,NT)
-                Y=jnp.concatenate([jnp.where(lane>row,R[:,:128],A[:,512:]),R[:,128:],R[:,:128]],axis=1)
-                S=S+Y+bias_scr[t]
-                m=jnp.max(S,axis=1,keepdims=True)
-                e=jnp.exp2((S-m)*(SC*LOG2E))
-                s=jnp.sum(e,axis=1,keepdims=True)
-                P=(e*(1.0/s)).astype(bf)
-                p_ref[p,t,h]=P
-                ctx.append(dot(P,vw,NN))
-            ctx_ref[p,pl.ds(off,128),:]=jnp.where(lane<64,ctx[0],ctx[1]).astype(bf)
-            keyside(c)
-            return c+1
-        lax.fori_loop(0,nblk,qblock,jnp.int32(5))
-        return c
-    lax.fori_loop(0,PAIRS,pair,0)
-
-def unskew(Grev):
-    return jnp.concatenate([pltpu.roll(Grev[8*g:8*g+8],384+8*g,1,stride=1,stride_axis=0) for g in range(16)],axis=0)
-
-def unrev(x, J):
-    hi=x.astype(bf); lo=(x-hi.astype(f32)).astype(bf)
-    y=dot(J,jnp.concatenate([hi,lo],axis=1))
-    return y[:,:128]+y[:,128:]
-
-def att_bwd_body(nblk, q_ref,k_ref,v_ref,krt_ref,qrt_ref,dctx_ref,p_ref,dq_ref,dk_ref,dv_ref,dkr_ref,dqr_ref,gt_scr,dvt_scr):
-    row=lax.broadcasted_iota(jnp.int32,(128,128),0); lane=lax.broadcasted_iota(jnp.int32,(128,128),1)
-    JR=(row+lane==127).astype(bf)
-    gt_scr[...]=jnp.zeros(gt_scr.shape,bf)
-    zero=jnp.zeros((128,128),bf)
-    def pair(p,c):
-        dvt_scr[...]=jnp.zeros(dvt_scr.shape,f32)
-        dkr_ref[p]=jnp.zeros((128,640),f32)
-        dqr_ref[p]=jnp.zeros((128,640),f32)
-        def qblock(t,J0):
-            off=pl.multiple_of(t*128,128)
-            qt=q_ref[p,pl.ds(off,128),:]
-            qT=qt.T
-            qTr=dot(qT,JR).astype(bf)
-            dct=dctx_ref[p,pl.ds(off,128),:]
-            dcT=dct.T
-            kw=k_ref[p,pl.ds(off,640),:]
-            vw=v_ref[p,pl.ds(off,640),:]
-            krt=krt_ref[p]
-            dq1=[]; dq2=[]
-            for h in range(2):
-                dp=dot(keep(dct,h),vw,NT)
-                Pb=p_ref[p,t,h]
-                Pf=Pb.astype(f32)
-                w=Pf*dp
-                inner=jnp.sum(w,axis=1,keepdims=True)
-                G=(w-Pf*inner).astype(bf)
-                Gd=jnp.where(lane==row,G[:,:128],zero)
-                Gm=jnp.concatenate([jnp.where(lane>row,G[:,:128],G[:,512:]),G[:,128:512]],axis=1)
-                Gu=unskew(dot(JR,Gm)).astype(bf)
-                dq1.append(dot(jnp.concatenate([G,Gd],axis=1),jnp.concatenate([kw,krt[512:]],axis=0)))
-                dq2.append(dot(Gu,krt[:512]))
-                hs=slice(64*h,64*h+64)
-                dkr_ref[p,hs,0:512]+=dot(qTr[hs],Gu)
-                dkr_ref[p,hs,512:640]+=dot(qT[hs],Gd)
-                dvt_scr[hs,pl.ds(off,640)]+=dot(dcT[hs],Pb)
-                for b in range(NB):
-                    gt_scr[h,J0+b,:,128*(4-b):128*(5-b)]=dot(JR,G[:,128*b:128*b+128],NT).astype(bf)
-            dq=jnp.where(lane<64,dq1[0],dq1[1])+unrev(jnp.where(lane<64,dq2[0],dq2[1]),JR)
-            dq_ref[p,pl.ds(off,128),:]=(SC*dq).astype(bf)
-            return J0+1
-        lax.fori_loop(0,nblk,qblock,jnp.int32(0))
-        def kblock(J,c):
-            off=pl.multiple_of(J*128,128)
-            kj=k_ref[p,pl.ds(off,128),:]
-            kT=kj.T
-            kTr=dot(kT,JR).astype(bf)
-            qw=jnp.concatenate([q_ref[p,pl.ds(pl.multiple_of(jnp.clip(J-4+w,0,nblk-1)*128,128),128),:] for w in range(NB)],axis=0)
-            rhs=jnp.concatenate([qw,qrt_ref[p]],axis=0)
-            dks=[]
-            for h in range(2):
-                GT=gt_scr[h,J]
-                Gd=jnp.where(lane+row==127,GT[:,:128],zero)
-                Gm=jnp.concatenate([jnp.where(lane+row>127,GT[:,:128],GT[:,512:]),GT[:,128:512]],axis=1).astype(f32)
-                Gu=unskew(Gm).astype(bf)
-                Gx=jnp.concatenate([Gu,Gd],axis=1)
-                dks.append(dot(jnp.concatenate([GT,Gx],axis=1),rhs))
-                hs=slice(64*h,64*h+64)
-                dqr_ref[p,hs,:]+=dot(kTr[hs],Gx)
-            dk_ref[p,pl.ds(off,128),:]=SC*unrev(jnp.where(lane<64,dks[0],dks[1]),JR)
-            dv_ref[p,pl.ds(off,128),:]=dvt_scr[:,pl.ds(off,128)].T
-            return c
-        lax.fori_loop(0,nblk+4,kblock,0)
-        dkr_ref[p]=SC*dkr_ref[p]
-        dqr_ref[p]=SC*dqr_ref[p]
-        return c
-    lax.fori_loop(0,PAIRS,pair,0)
-
-def att_bwd(q,k,v,krt,qrt,dctx,P):
-    T=q.shape[1]; nblk=T//128; E=T+512
-    return pl.pallas_call(functools.partial(att_bwd_body,nblk),
-        out_shape=[jax.ShapeDtypeStruct((PAIRS,T,128),bf),jax.ShapeDtypeStruct((PAIRS,E,128),f32),jax.ShapeDtypeStruct((PAIRS,E,128),f32),
-          jax.ShapeDtypeStruct((PAIRS,128,640),f32),jax.ShapeDtypeStruct((PAIRS,128,640),f32)],
-        scratch_shapes=[pltpu.VMEM((2,nblk+4,128,640),bf),pltpu.VMEM((128,E),f32)],
-        compiler_params=pltpu.CompilerParams(vmem_limit_bytes=48<<20),
-    )(q,k,v,krt,qrt,dctx,P)
+                gt_scr[slot + b, h, 16 * (i % 8) : 16 * (i % 8) + 16, 128 * (4 - b) : 128 * (5 - b)] = Gb[:, 128 * h : 128 * h + 128]
+            return G
+
+        ends = None
+        final = None
+        for i in range(32):
+            G = grad(i)
+            if i < 8:
+                at = row16 + 16 * i - lane16 % 128
+                part = jnp.where(at == 0, G, 0.0)
+                part = part[:8] + part[8:]
+                ends = part if ends is None else ends + part
+                other = grad(32 + i)
+                part = jnp.where(at == 0, other, 0.0)
+                part = part[:8] + part[8:]
+                final = part if final is None else final + part
+                G = jnp.where(at > 0, G, other)
+            gm_scr[16 * i : 16 * i + 16, :] = G
+        ends = jnp.sum(ends, axis=0, keepdims=True)
+        final = jnp.sum(final, axis=0, keepdims=True)
+        final = jnp.concatenate([jnp.broadcast_to(final[:, :128], (64, 128)), jnp.broadcast_to(final[:, 128:], (64, 128))], axis=0)
+        dqr_ref[p, :, 512:640] += kT_ref[p, :, tile(t + 4)].astype(f32) * final
+        dkc_ref[p, tile(t + 4), :] += (qend_ref[p].astype(f32) * final).T
+        dv_ref[p, window(t), :] += dot(p_ref[p, t], (D2.astype(f32) * inv).astype(bf).T)
+        for h in range(2):
+            cols = slice(128 * h, 128 * h + 128)
+            held = None
+            for i, y in stream_rows(lambda i: gm_scr[8 * i : 8 * i + 8, cols], True, (1, 2, 4)):
+                if i == 0:
+                    y = y + jnp.where(row[:8] == 1, ends[:, cols], 0.0)
+                if i % 2 == 1:
+                    held = y
+                else:
+                    gu[8 * i : 8 * i + 16, cols] = jnp.concatenate([y, held], axis=0).astype(bf)
+
+    def downstream(n, gb, gu):
+        n = jnp.maximum(n, 0)
+        p, t = n // nblk, n % nblk
+        dqT = own_heads(dot(kT_ref[p, :, window(t)], gb[...]) + dot(krtT_ref[p], gu[...]))
+        dq_ref[p, tile(t), :] = (SC * dqT).astype(bf).T
+        Qm = tall_diagonal(q_ref[p, tile(t), :])
+        dkc_ref[p, window(t), :] += dot(gb[...], Qm)
+        dkr_ref[p] += dot(gu[...], Qm)
+
+    def body(m, slot, late):
+        p = m // half
+        if late:
+            kblocks(p - 1, per * (m % half), (1 - p % 2) * keys)
+        downstream(2 * m - 1, gb1, gu1)
+        upstream(2 * m, slot, gb0, gu0)
+        downstream(2 * m, gb0, gu0)
+        upstream(2 * m + 1, slot + 1, gb1, gu1)
+        following = slot + 2
+        following = jnp.where(following == nblk, keys, following)
+        return jnp.where(following == keys + nblk, 0, following)
+
+    slot = lax.fori_loop(0, half, lambda m, slot: body(m, slot, False), jnp.int32(0))
+    lax.fori_loop(half, items // 2, lambda m, slot: body(m, slot, True), slot)
+    downstream(items - 1, gb1, gu1)
+
+    def last(i, carry):
+        kblocks(PAIRS - 1, per * i, ((PAIRS - 1) % 2) * keys)
+        return carry
+
+    lax.fori_loop(0, half, last, 0)
 
 
 def vector(vec_ref, name):
@@ -559,28 +714,43 @@
     return jnp.concatenate([dot(JR, values[128 * b : 128 * b + 128]).astype(bf) for b in reversed(range(blocks))], axis=0)
 
 
-def project_body(x_ref, query_w, key_w, value_w, table_ref, vec_ref, q_ref, k_ref, v_ref, krt_ref, qrt_ref, pos_ref):
+def project_body(x_ref, query_w, key_w, value_w, table_ref, vec_ref, q_ref, qT_ref, k_ref, kT_ref, kTr_ref, v_ref, vT_ref, krt_ref, krtT_ref, qrt_ref, qrtT_ref, pos_ref):
     tokens = q_ref.shape[1]
     JR = reversal()
+    lane = iotas(512, 128)[1]
     unit, _ = normalized(table_ref[...].astype(f32))
     pos = (unit * vector(vec_ref, "rel_gain") + vector(vec_ref, "rel_shift")).astype(bf)
-    pos_rev = reversed_rows(pos, JR)
-    pos_ref[...] = pos_rev
-    for w, b, out in ((key_w, "key_b", krt_ref), (query_w, "query_b", qrt_ref)):
-        table = (dot(pos_rev, w[...]) + vector(vec_ref, b)).astype(bf)
-        for p in range(PAIRS):
-            out[p, 0:512, :] = table[:, 128 * p : 128 * p + 128]
-            out[p, 512:640, :] = jnp.broadcast_to(table[0:1, 128 * p : 128 * p + 128], (128, 128))
-
+    pos = pltpu.roll(reversed_rows(pos, JR).astype(f32), 1, 0).astype(bf)
+    pos_ref[...] = pos
+    keys = dot(pos, key_w[...]) + vector(vec_ref, "key_b")
+    moved = pltpu.roll(keys, 1, 0).astype(bf)
+    keys = keys.astype(bf)
+    queries = (dot(pos, query_w[...]) + vector(vec_ref, "query_b")).astype(bf)
+    for p in range(PAIRS):
+        cols = slice(128 * p, 128 * p + 128)
+        krt_ref[p] = keys[:, cols]
+        krt_ref[PAIRS + p] = moved[:, cols]
+        krtT_ref[p] = keys[:, cols].T
+        qrtT_ref[p, :, 0:512] = queries[:, cols].T
+        qrtT_ref[p, :, 512:640] = jnp.broadcast_to(queries[1:2, cols], (128, 128)).T
+        zero = jnp.zeros((512, 128), bf)
+        qrt_ref[p, 0:512, :] = jnp.where(lane < 64, queries[:, cols], zero)
+        qrt_ref[p, 512:1024, :] = jnp.where(lane < 64, zero, queries[:, cols])
     bias = {name: vector(vec_ref, name) for name in ("query_b", "key_b", "value_b")}
 
     def chunk(i, carry):
         rows = pl.ds(pl.multiple_of(i * 256, 256), 256)
         x = x_ref[rows, :]
-        for w, b, out in ((key_w, "key_b", k_ref), (value_w, "value_b", v_ref)):
-            y = (dot(x, w[...]) + bias[b]).astype(bf)
-            for p in range(PAIRS):
-                out[p, rows, :] = y[:, 128 * p : 128 * p + 128]
+        y = (dot(x, key_w[...]) + bias["key_b"]).astype(bf)
+        w = (dot(x, value_w[...]) + bias["value_b"]).astype(bf)
+        for p in range(PAIRS):
+            cols = slice(128 * p, 128 * p + 128)
+            k_ref[p, rows, :] = y[:, cols]
+            turned = y[:, cols].T
+            kT_ref[p, :, rows] = turned
+            kTr_ref[p, :, rows] = jnp.concatenate([dot(turned[:, :128], JR), dot(turned[:, 128:], JR)], axis=1).astype(bf)
+            v_ref[p, rows, :] = w[:, cols]
+            vT_ref[p, :, rows] = w[:, cols].T
         return carry
 
     lax.fori_loop(0, x_ref.shape[0] // 256, chunk, 0)
@@ -591,6 +761,7 @@
         y = (dot(x, query_w[...]) + bias["query_b"]).astype(bf)
         for p in range(PAIRS):
             q_ref[p, rows, :] = y[:, 128 * p : 128 * p + 128]
+            qT_ref[p, :, rows] = y[:, 128 * p : 128 * p + 128].T
         return carry
 
     lax.fori_loop(0, tokens // 256, own, 0)
@@ -652,7 +823,7 @@
         add_vector(dvec_ref, "output_b", column_sum(dattn.astype(f32)))
         dctx = dot(dattn, output_w[...], NT).astype(bf)
         for p in range(PAIRS):
-            dctx_ref[p, rows, :] = dctx[:, 128 * p : 128 * p + 128]
+            dctx_ref[p, :, rows] = dctx[:, 128 * p : 128 * p + 128].T
         return carry
 
     lax.fori_loop(0, tokens // C, chunk, 0)
@@ -692,11 +863,16 @@
 
 def tail_table(dkr_ref, dqr_ref, pos_ref, table_ref, vec_ref, query_w, key_w, dwq_ref, dwk_ref, dtable_ref, dvec_ref):
     JR = reversal()
-    first = lax.broadcasted_iota(jnp.int32, (512, 384), 0) == 0
+    second = iotas(512, 128)[0] == 1
+    tabs = {"key_b": jnp.concatenate([SC * dkr_ref[p] for p in range(PAIRS)], axis=1)}
+    parts = []
+    for p in range(PAIRS):
+        part = dqr_ref[p].T
+        parts.append(SC * (part[:512] + jnp.where(second, column_sum(part[512:]), 0.0)))
+    tabs["query_b"] = jnp.concatenate(parts, axis=1)
     dpos = None
-    for ref, w, dw, name in ((dkr_ref, key_w, dwk_ref, "key_b"), (dqr_ref, query_w, dwq_ref, "query_b")):
-        halves = jnp.concatenate([ref[p].T for p in range(PAIRS)], axis=1)
-        tab = halves[:512] + jnp.where(first, column_sum(halves[512:]), 0.0)
+    for w, dw, name in ((key_w, dwk_ref, "key_b"), (query_w, dwq_ref, "query_b")):
+        tab = tabs[name]
         if name == "key_b":
             dw[...] = dot2(pos_ref[...], tab, TN)
             put_vector(dvec_ref, name, column_sum(tab))
@@ -705,21 +881,23 @@
             add_vector(dvec_ref, name, column_sum(tab))
         part = dot2(tab, w[...], NT)
         dpos = part if dpos is None else dpos + part
-    unit, inverse = normalized(jnp.concatenate([dot(JR, table_ref[128 * b : 128 * b + 128, :]) for b in reversed(range(4))], axis=0))
+    table = jnp.concatenate([dot(JR, table_ref[128 * b : 128 * b + 128, :]) for b in reversed(range(4))], axis=0)
+    unit, inverse = normalized(pltpu.roll(table, 1, 0))
     put_vector(dvec_ref, "rel_gain", column_sum(dpos * unit))
     put_vector(dvec_ref, "rel_shift", column_sum(dpos))
-    dpos = norm_back(dpos, vector(vec_ref, "rel_gain"), unit, inverse).astype(bf)
+    dpos = pltpu.roll(norm_back(dpos, vector(vec_ref, "rel_gain"), unit, inverse), 511, 0).astype(bf)
     for b in range(4):
         dtable_ref[128 * b : 128 * b + 128, :] = dot(JR, dpos[128 * (3 - b) : 128 * (4 - b)])
 
 
-def tail_keys(dk_ref, dv_ref, halo_ref, x_ref, key_w, value_w, dx_ref, dwk_ref, dwv_ref, dvec_ref):
+def tail_keys(dkc_ref, dkp_ref, dv_ref, halo_ref, x_ref, key_w, value_w, dx_ref, dwk_ref, dwv_ref, dvec_ref):
     tokens = dx_ref.shape[0]
     x = x_ref[SPAN : SPAN + tokens, :]
-    for which, (ref, w, dw, name) in enumerate(((dk_ref, key_w, dwk_ref, "key_b"), (dv_ref, value_w, dwv_ref, "value_b"))):
+    for which, (ref, w, dw, name) in enumerate(((None, key_w, dwk_ref, "key_b"), (dv_ref, value_w, dwv_ref, "value_b"))):
         pieces = []
         for p in range(PAIRS):
-            own = ref[p, SPAN : SPAN + tokens, :]
+            middle = slice(SPAN, SPAN + tokens)
+            own = SC * (dkc_ref[p, middle, :] + dkp_ref[p, middle, :]) if ref is None else ref[p, middle, :]
             edge = [halo_ref[side, which, p].astype(f32) for side in (0, 1)]
             pieces.append(jnp.concatenate([own[:SPAN] + edge[0], own[SPAN : tokens - SPAN], own[tokens - SPAN :] + edge[1]], axis=0).astype(bf))
         d = jnp.concatenate(pieces, axis=1)
@@ -872,27 +1050,57 @@
     )(slot, x, seg)
 
 
-def forward_kernel(x_ref, seg_ref, query_w, key_w, value_w, table_ref, vec_ref, q_ref, k_ref, v_ref, krt_ref, qrt_ref, pos_ref, ctx_ref, p_ref, x_scr, bias_scr):
-    project_body(x_ref, query_w, key_w, value_w, table_ref, vec_ref, q_ref, k_ref, v_ref, krt_ref, qrt_ref, pos_ref)
-    att_fwd_body(q_ref.shape[1] // 128, q_ref, k_ref, v_ref, krt_ref, qrt_ref, seg_ref, ctx_ref, p_ref, x_scr, bias_scr)
+def projected(T):
+    shape = jax.ShapeDtypeStruct
+    E = T + 2 * SPAN
+    natural = {"q": (T, 128), "qT": (128, T), "k": (E, 128), "kT": (128, E), "kTr": (128, E), "v": (E, 128), "vT": (128, E)}
+    tables = {"krt": (512, 128), "krtT": (128, 512), "qrt": (1024, 128), "qrtT": (128, 640)}
+    out = {name: shape((PAIRS,) + extent, bf) for name, extent in (natural | tables).items()}
+    out["krt"] = shape((2 * PAIRS, 512, 128), bf)
+    out["pos"] = shape((512, D), bf)
+    out["ctx"] = shape((PAIRS, T, 128), bf)
+    out["e"] = shape((PAIRS, T // 128, 640, 256), bf)
+    out["inv"] = shape((PAIRS, T // 128, 8, 256), f32)
+    return out
+
+
+def forward_kernel(x_ref, seg_ref, query_w, key_w, value_w, table_ref, vec_ref, *refs):
+    names = list(projected(128))
+    outs = dict(zip(names, refs))
+    project_body(x_ref, query_w, key_w, value_w, table_ref, vec_ref, *[outs[n] for n in names[:12]])
+    att_fwd_body(outs["q"].shape[1] // 128, outs["qT"], outs["k"], outs["vT"], outs["krt"], outs["qrtT"], seg_ref, outs["ctx"], outs["e"], outs["inv"], *refs[len(names) :])
 
 
 def forward(x_ext, seg_ext, query_w, key_w, value_w, table, vec):
-    E = x_ext.shape[0]
-    T = E - 2 * SPAN
+    T = x_ext.shape[0] - 2 * SPAN
     blocks = T // 128
+    outs = projected(T)
+    results = pl.pallas_call(
+        forward_kernel,
+        out_shape=list(outs.values()),
+        in_specs=[VMEM] * 7,
+        out_specs=[VMEM] * len(outs),
+        scratch_shapes=[pltpu.VMEM((2 * (blocks + 4), 2, 128, 640), bf), pltpu.VMEM((blocks, 640, 128), f32)]
+        + [pltpu.VMEM((640, 256), f32)] * 2 + [pltpu.VMEM((512, 256), f32)] * 2 + [pltpu.VMEM((640, 256), f32)] * 2 + [pltpu.VMEM((8, 256), f32)] * 2,
+        compiler_params=pltpu.CompilerParams(vmem_limit_bytes=60 << 20),
+    )(x_ext, seg_ext, query_w, key_w, value_w, table, vec)
+    return dict(zip(outs, results))
+
+
+def backward(f, dctxT):
+    T = dctxT.shape[2]
+    E, blocks = T + 2 * SPAN, T // 128
     shape = jax.ShapeDtypeStruct
+    accumulator = shape((PAIRS, E, 128), f32)
     return pl.pallas_call(
-        forward_kernel,
-        out_shape=[
-            shape((PAIRS, T, 128), bf), shape((PAIRS, E, 128), bf), shape((PAIRS, E, 128), bf), shape((PAIRS, 640, 128), bf),
-            shape((PAIRS, 640, 128), bf), shape((512, D), bf), shape((PAIRS, T, 128), bf), shape((PAIRS, blocks, 2, 128, 640), bf),
-        ],
-        in_specs=[VMEM] * 7,
-        out_specs=[VMEM] * 8,
-        scratch_shapes=[pltpu.VMEM((2, blocks + 5, 128, 640), bf), pltpu.VMEM((blocks, 128, 640), f32)],
-        compiler_params=pltpu.CompilerParams(vmem_limit_bytes=56 << 20),
-    )(x_ext, seg_ext, query_w, key_w, value_w, table, vec)
+        functools.partial(att_bwd_body, blocks),
+        out_shape=[shape((PAIRS, T, 128), bf), accumulator, accumulator, accumulator, shape((PAIRS, 512, 128), f32), shape((PAIRS, 128, 640), f32)],
+        in_specs=[VMEM] * 10,
+        out_specs=[VMEM] * 6,
+        scratch_shapes=[pltpu.VMEM((2 * (blocks + 4), 2, 128, 640), bf), pltpu.VMEM((640, 256), f32), pltpu.VMEM((512, 256), f32)]
+        + [pltpu.VMEM((640, 256), bf)] * 2 + [pltpu.VMEM((512, 256), bf)] * 2,
+        compiler_params=pltpu.CompilerParams(vmem_limit_bytes=60 << 20),
+    )(f["q"], f["kT"], f["kTr"], f["v"], f["krtT"], f["qrt"], f["qrtT"][:, :, 512:], dctxT, f["e"], f["inv"])
 
 
 def feed_kernel(x_ref, ctx_ref, og_ref, output_w, up_w, down_w, vec_ref, out_ref, dz1_ref, dctx_ref, dflat_ref, dvec_ref, ml, dup, act, ddown, dattn, slope, wide):
@@ -905,7 +1113,7 @@
     shape = jax.ShapeDtypeStruct
     return pl.pallas_call(
         feed_kernel,
-        out_shape=[shape((T, D), bf), shape((T, D), f32), shape((PAIRS, T, 128), bf), shape((FEED_ROWS, 128), bf), shape(vec.shape, f32)],
+        out_shape=[shape((T, D), bf), shape((T, D), f32), shape((PAIRS, 128, T), bf), shape((FEED_ROWS, 128), bf), shape(vec.shape, f32)],
         in_specs=[VMEM] * 7,
         out_specs=[VMEM] * 5,
         scratch_shapes=[
@@ -916,7 +1124,7 @@
     )(x_ext, ctx, out_grad, output_w, up_w, down_w, vec)
 
 
-def tail_kernel(grid, shard, dq_ref, dk_ref, dv_ref, dkr_ref, dqr_ref, dz1_ref, x_ref, pos_ref, table_ref, vec_ref, query_w, key_w, value_w, dflat_ref, dvec_in,
+def tail_kernel(grid, shard, dq_ref, dkc_ref, dkp_ref, dv_ref, dkr_ref, dqr_ref, dz1_ref, x_ref, pos_ref, table_ref, vec_ref, query_w, key_w, value_w, dflat_ref, dvec_in,
                 dx_ref, sum_ref, dvec_ref, dwq, dwk, dwv, dtable, wide, flat, kids, outgoing, total, halo_out, halo_in, send_sem, recv_sem, halo_send, halo_recv):
     p = grid.here()
     tokens = dx_ref.shape[0]
@@ -925,8 +1133,8 @@
     enter_all(grid, p)
     rims = (pl.ds(0, SPAN), pl.ds(tokens + SPAN, SPAN))
     for side in (0, 1):
-        for which, ref in ((0, dk_ref), (1, dv_ref)):
-            halo_out[side, which] = ref[:, rims[side], :].astype(bf)
+        halo_out[side, 0] = (SC * (dkc_ref[:, rims[side], :] + dkp_ref[:, rims[side], :])).astype(bf)
+        halo_out[side, 1] = dv_ref[:, rims[side], :].astype(bf)
 
     def halo_copy(side):
         return remote(halo_out.at[side], halo_in.at[1 - side], halo_send.at[side], halo_recv.at[1 - side], beside(grid, -1 if side == 0 else 1))
@@ -946,7 +1154,7 @@
     pl.when(after)(lambda: halo_copy(1).wait_send())
     pl.when(before)(lambda: halo_copy(1).wait_recv())
     pl.when(after)(lambda: halo_copy(0).wait_recv())
-    tail_keys(dk_ref, dv_ref, halo_in, x_ref, key_w, value_w, dx_ref, dwk, dwv, dvec_ref)
+    tail_keys(dkc_ref, dkp_ref, dv_ref, halo_in, x_ref, key_w, value_w, dx_ref, dwk, dwv, dvec_ref)
     place = matrix_rows()
     rest = flat.shape[0] - FEED_FIRST - FEED_ROWS
     wide[FEED_FIRST:, :] = jnp.zeros((rest, 128), f32)
@@ -968,13 +1176,13 @@
 def tail(grid, shard, *args):
     _, groups = shard_groups(shard, grid.count)
     rows = flat_rows(shard, grid.count)
-    tokens = args[5].shape[0]
+    tokens = args[6].shape[0]
     names, half = len(direction_names(grid)), grid.count // 2
     shape = jax.ShapeDtypeStruct
     dx, summed, _ = pl.pallas_call(
         functools.partial(tail_kernel, grid, shard),
         out_shape=[shape((tokens, D), f32), shape((16 * groups, 128), f32), shape((vector_rows()[1], 128), f32)],
-        in_specs=[VMEM] * 15,
+        in_specs=[VMEM] * 16,
         out_specs=[VMEM] * 3,
         scratch_shapes=[
             pltpu.VMEM((D, D), f32), pltpu.VMEM((D, D), f32), pltpu.VMEM((D, D), f32), pltpu.VMEM((2 * SPAN, D), f32),
@@ -1005,10 +1213,10 @@
     seg = jnp.broadcast_to(segment_ids + 1, (8, tokens_here))
     *matrices, vec, x_ext, seg_ext = gather_params(grid, shard, slot, layer_input[0], seg)
     query_w, key_w, value_w, output_w, up_w, down_w, table = matrices
-    q, k, v, krt, qrt, pos, ctx, probs = forward(x_ext, seg_ext, query_w, key_w, value_w, table, vec)
-    block_output, dz1, dctx, dflat, dvec = feed(x_ext, ctx, out_grad[0], output_w, up_w, down_w, vec)
-    dq, dk, dv, dkr, dqr = att_bwd(q, k, v, krt, qrt, dctx, probs)
-    dx, summed = tail(grid, shard, dq, dk, dv, dkr, dqr, dz1, x_ext, pos, table, vec, query_w, key_w, value_w, dflat, dvec)
+    f = forward(x_ext, seg_ext, query_w, key_w, value_w, table, vec)
+    block_output, dz1, dctxT, dflat, dvec = feed(x_ext, f["ctx"], out_grad[0], output_w, up_w, down_w, vec)
+    summed_up = backward(f, dctxT)
+    dx, summed = tail(grid, shard, *summed_up, dz1, x_ext, f["pos"], table, vec, query_w, key_w, value_w, dflat, dvec)
     weight_grad = lax.dynamic_slice(summed.reshape(-1), (shift,), (shard,))
     all_tokens = tokens_here * grid.seq * layer_input.shape[0] * grid.row
     rate = 0.1 / math.sqrt(all_tokens)

time: 237 us -> 205 us (0.86)
  Pallas kernels: 216 us -> 186 us
    pallas_call x2, Pallas kernels: 115 us -> 84.4 us  [the longest x1 46.6 us: backward(): pl.pallas_call(functools.partial(att_bwd_body, blocks), out_shape=[shape(...]
    unnamed x47 -> x33, local copies, waits for them, and re-layouts: 14.2 us -> 10.3 us
where the time goes in v1:
time: 205 us
  Pallas kernels  186 us (91%)
  local copies, waits for them, and re-layouts  13.1 us (6%)
  other arithmetic  4.45 us (2%)
    pallas_call x1, Pallas kernels, backward(): pl.pallas_call(functools.partial(att_bwd_body, blocks), out_shape=[shape(...  46.6 us
    pallas_call x1, Pallas kernels, tail(): pl.pallas_call(functools.partial(tail_kernel, grid, shard), out_shape=[sh...  46.6 us
    pallas_call x1, Pallas kernels, forward(): pl.pallas_call(forward_kernel, out_shape=list(outs.values()), in_specs=[V...  37.8 us
    pallas_call x1, Pallas kernels, gather_params(): pl.pallas_call(functools.partial(gather_kernel, grid, shard), out_shape=m...  34.9 us
    pallas_call x1, Pallas kernels, feed(): pl.pallas_call(feed_kernel, out_shape=[shape((T, D), bf), shape((T, D), f...  20.5 us
    unnamed x33, local copies, waits for them, and re-layouts  10.3 us

profile of v1, /device:TPU:0, one launch (start us, length us, event | category | flops | bytes accessed | tf_op | source)
XLA Modules:
  0.0 204.7 jit_solution(10596129596980786226)
XLA Ops:
  0.7 0.7 broadcast_add_fusion
  1.4 1.0 convert_element_type.6
  2.3 1.2 dynamic_update_slice.3
  3.5 0.0 copy-start.7
  3.6 1.1 copy-done.7
  4.7 34.9 %shard_map.117 = (bf16[384,384]{1,0:T(8,128)(2,1)S(1)}, bf16[384,384]{1,0:T(8,128)(2,1)S(1)}, bf16[384,384]{1,0:T(8,128)(2,1)S(1)}, bf16[384,384]{1,0:T(8,128)(2...) custom-call(bf16[512,128]{1,0:T(8,128)(2,1)S(1)} %bitcast.8, ...), custom_call_target="tpu_custom_call" | custom-call | tf_op jit(solution)/shard_map/pallas_call | solution.py:1030
  39.6 0.0 copy-start
  39.6 1.0 copy-done
  40.7 0.0 copy-start.1
  40.7 0.8 copy-done.1
  41.4 0.0 copy-start.2
  41.4 1.0 copy-done.2
  42.4 0.0 copy-start.3
  42.4 1.1 copy-done.3
  43.5 0.0 copy-start.4
  43.5 0.7 copy-done.4
  44.2 0.0 copy-start.5
  44.2 0.7 copy-done.5
  45.0 0.0 copy-start.6
  45.0 0.7 copy-done.6
  45.7 0.0 copy-start.8
  45.7 0.7 copy-done.8
  46.4 0.0 copy-start.9
  46.4 0.6 copy-done.9
  47.0 0.0 copy-start.10
  47.0 0.6 copy-done.10
  47.6 37.8 %shard_map.118 = (bf16[3,1024,128]{2,1,0:T(8,128)(2,1)}, bf16[3,128,1024]{2,1,0:T(8,128)(2,1)}, bf16[3,1536,128]{2,1,0:T(8,128)(2,1)}, bf16[3,128,1536]{2,1,0:T(...) custom-call(bf16[1536,384]{1,0:T(8,128)(2,1)} %copy-done, ...), custom_call_target="tpu_custom_call" | custom-call | tf_op jit(solution)/shard_map/pallas_call | solution.py:1078
  85.5 1.5 slice.3.qend_ref
  87.0 20.5 %shard_map.119 = (bf16[1024,384]{1,0:T(8,128)(2,1)}, f32[1024,384]{1,0:T(8,128)}, bf16[3,128,1024]{2,1,0:T(8,128)(2,1)}, bf16[10368,128]{1,0:T(8,128)(2,1)}, f32[48,128]{1,0:T(8,128)}) custom-call(bf16[1536,384]{1,0:T(8,128)(2,1)} %copy-done, bf16[3,1024,128]{2,1,0:T(8,128)(2,1)} %get-tuple-element.48.ctx_ref, bf16[1024,384]{1,0:T(8,128)(2,1)} %bitcast.10, ...), custom_call_target="tpu_custom_call" | custom-call | tf_op jit(solution)/shard_map/pallas_call | solution.py:1114
  107.5 46.6 %shard_map.120 = (bf16[3,1024,128]{2,1,0:T(8,128)(2,1)}, f32[3,1536,128]{2,1,0:T(8,128)}, f32[3,1536,128]{2,1,0:T(8,128)}, f32[3,1536,128]{2,1,0:T(8,128)}, f32[...) custom-call(bf16[3,1024,128]{2,1,0:T(8,128)(2,1)} %get-tuple-element.53.q_ref, ...), custom_call_target="tpu_custom_call" | custom-call | tf_op jit(solution)/shard_map/pallas_call | solution.py:1095
  154.1 0.0 copy-start.12
  154.1 0.0 copy-start.14
  154.1 0.0 copy-start.15
  154.1 46.6 %shard_map.121 = (f32[1024,384]{1,0:T(8,128)}, f32[512,128]{1,0:T(8,128)}, f32[48,128]{1,0:T(8,128)}) custom-call(bf16[3,1024,128]{2,1,0:T(8,128)(2,1)} %get-tuple-element.63.dq_ref, f32[3,1536,128]{2,1,0:T(8,128)} %get-tuple-element.64.dkc_ref, f32[3,1536,128]{2,1,0:T(8,128)} %get-tuple-element.65.dkp_ref, f32[3,1536,128]{2,1,0:T(8,128)} %get-tuple-element.66.dv_ref, ...), custom_call_target="tpu_custom_call" | custom-call | tf_op jit(solution)/shard_map/pallas_call | solution.py:1182
  200.7 0.0 copy-start.11
  200.7 0.0 copy-done.12
  200.7 0.0 copy-done.14
  200.8 2.0 fusion
  202.8 0.0 copy-start.13
  202.8 0.0 copy-done.15
  202.8 0.8 add_multiply_fusion
  203.6 0.0 copy-done.11
  203.6 1.1 copy.15
  204.7 0.0 copy-done.13
  (2 shorter events, 0.0 us)
Async XLA Ops:
  3.5 1.1 copy-start.7
  39.6 1.0 copy-start
  40.7 0.8 copy-start.1
  41.4 1.0 copy-start.2
  42.4 1.1 copy-start.3
  43.5 0.7 copy-start.4
  44.2 0.7 copy-start.5
  45.0 0.7 copy-start.6
  45.7 0.7 copy-start.8
  46.4 0.6 copy-start.9
  47.0 0.6 copy-start.10
  154.1 46.6 %copy-start.12 = (f32[61620]{0:T(1024)S(1)}, f32[61620]{0:T(1024)}, u32[]{:S(2)}) copy-start(f32[61620]{0:T(1024)} %param.9) | copy-start | bytes 739444
  154.1 46.6 %copy-start.14 = (f32[61620]{0:T(1024)S(1)}, f32[61620]{0:T(1024)}, u32[]{:S(2)}) copy-start(f32[61620]{0:T(1024)} %param.10) | copy-start | bytes 739444
  154.1 48.7 %copy-start.15 = (f32[61620]{0:T(1024)S(1)}, f32[61620]{0:T(1024)}, u32[]{:S(2)}) copy-start(f32[61620]{0:T(1024)} %param.11) | copy-start | bytes 739444
  200.7 2.8 %copy-start.11 = (f32[1024,384]{1,0:T(8,128)S(1)}, f32[1024,384]{1,0:T(8,128)}, u32[]{:S(2)}) copy-start(f32[1024,384]{1,0:T(8,128)} %get-tuple-element.73) | copy-start | bytes 4718596
  202.8 1.9 copy-start.13
